TPU v7x, 32 devices: a whole 2x2x4 slice. The times are simulated.
32 devices in a mesh: group: 4 (over z), dev: 8 (over y, x, core).
Axes of the slice: x: 2, y: 2, z: 4, core: 2. Of those that a mesh axis runs over, the one named last changes fastest.
Arguments:
- blocks_in: float32 [992, 8, 4096], P(('group', 'dev')), as said below
- counts: int32 [32], P(('group', 'dev')), may hold values from 1 to 31, as said below
Outputs:
- blocks_out: float32 [512, 8, 4096], P(('group', 'dev'))
Inputs may be any that keep to these rules, and one draw needn't show every extreme that they name: `blocks_in`: every slot holds a state of positive density and pressure. Device i (in the order of group+dev) holds its live meshblocks in its first counts[i] slots, in curve order. The counts sum to 512; for every device i, starts[i] - i * 16 lies in 0 .. 15.
All inputs are finite; a program needn't handle non-finite values.
Results may differ from a plain program's by a relative error of at most 0.0003.
Values sent between devices are 32-bit elements; how exact they have to be, the bound alone decides.
A program may use at most 192 MiB of HBM per device.

v0:
```python
import jax
import jax.numpy as jnp
from jax import lax
from jax.sharding import PartitionSpec as P

BS = 16
BRICK_Y = 2
BRICK_Z = 8
BRICK_X = 1
BLK_DEV = 16


GAMMA = 5.0 / 3.0
COURANT = 0.25
DENSITY_FLOOR = 0.05
PRESSURE_FLOOR = 0.05


def with_halo(cells, sides, width):
    for axis, dim in sides:
        count = lax.axis_size(axis)
        head = lax.slice_in_dim(cells, 0, width, axis=dim)
        tail = lax.slice_in_dim(cells, cells.shape[dim] - width, cells.shape[dim], axis=dim)
        cells = jnp.concatenate(
            [
                lax.ppermute(tail, axis, [(i, (i + 1) % count) for i in range(count)]),
                cells,
                lax.ppermute(head, axis, [((i + 1) % count, i) for i in range(count)]),
            ],
            axis=dim,
        )
    return cells


def passed_along(value, axis, steps):
    count = lax.axis_size(axis)
    first, last = (max(0, -steps), min(count, count - steps))
    return lax.ppermute(value, axis, [(source, source + steps) for source in range(first, last)])


def trimmed(values, along, front, back):
    return lax.slice_in_dim(values, front, values.shape[along] - back, axis=along)


def primitive(state):
    density = jnp.maximum(state[0], DENSITY_FLOOR)
    velocity = state[1:4] / density
    magnetic = state[5:8]
    kinetic = 0.5 * density * jnp.sum(velocity * velocity, axis=0)
    magnetic_energy = 0.5 * jnp.sum(magnetic * magnetic, axis=0)
    pressure = jnp.maximum((GAMMA - 1.0) * (state[4] - kinetic - magnetic_energy), PRESSURE_FLOOR)
    return jnp.concatenate([density[None], velocity, pressure[None], magnetic], axis=0)


def conserved(prims):
    density = prims[0]
    velocity = prims[1:4]
    magnetic = prims[5:8]
    energy = (
        prims[4] / (GAMMA - 1.0)
        + 0.5 * density * jnp.sum(velocity * velocity, axis=0)
        + 0.5 * jnp.sum(magnetic * magnetic, axis=0)
    )
    return jnp.concatenate([density[None], density * velocity, energy[None], magnetic], axis=0)


def fast_speed(prims, normal):
    density = prims[0]
    sound = GAMMA * prims[4] / density
    alfven = jnp.sum(prims[5:8] * prims[5:8], axis=0) / density
    along_field = prims[5 + normal] * prims[5 + normal] / density
    total = sound + alfven
    root = jnp.sqrt(jnp.maximum(total * total - 4.0 * sound * along_field, 0.0))
    return jnp.sqrt(0.5 * (total + root))


def physical_flux(prims, state, normal):
    density = prims[0]
    velocity = prims[1:4]
    magnetic = prims[5:8]
    speed_normal = velocity[normal]
    field_normal = magnetic[normal]
    total_pressure = prims[4] + 0.5 * jnp.sum(magnetic * magnetic, axis=0)
    unit_normal = jnp.array(
        [1.0 if component == normal else 0.0 for component in range(3)], dtype=jnp.float32
    )
    unit_normal = unit_normal.reshape((3,) + (1,) * (velocity.ndim - 1))
    momentum_flux = (
        density * velocity * speed_normal - magnetic * field_normal + unit_normal * total_pressure
    )
    energy_flux = (state[4] + total_pressure) * speed_normal - field_normal * jnp.sum(
        velocity * magnetic, axis=0
    )
    induction = speed_normal * magnetic - velocity * field_normal
    return jnp.concatenate(
        [(density * speed_normal)[None], momentum_flux, energy_flux[None], induction], axis=0
    )


def hlle_flux(left, right, normal):
    state_left = conserved(left)
    state_right = conserved(right)
    flux_left = physical_flux(left, state_left, normal)
    flux_right = physical_flux(right, state_right, normal)
    fast_left = fast_speed(left, normal)
    fast_right = fast_speed(right, normal)
    upper = jnp.maximum(
        jnp.maximum(right[1 + normal] + fast_right, left[1 + normal] + fast_left), 0.0
    )
    lower = jnp.minimum(
        jnp.minimum(left[1 + normal] - fast_left, right[1 + normal] - fast_right), 0.0
    )
    return (upper * flux_left - lower * flux_right + upper * lower * (state_right - state_left)) / (
        upper - lower
    )


def minmod(first, second):
    return 0.5 * (jnp.sign(first) + jnp.sign(second)) * jnp.minimum(jnp.abs(first), jnp.abs(second))


def divergence(prims, along, normal):
    backward = trimmed(prims, along, 1, 1) - trimmed(prims, along, 0, 2)
    forward = trimmed(prims, along, 2, 0) - trimmed(prims, along, 1, 1)
    slope = minmod(backward, forward)
    left = trimmed(prims, along, 1, 2) + 0.5 * trimmed(slope, along, 0, 1)
    right = trimmed(prims, along, 2, 1) - 0.5 * trimmed(slope, along, 1, 0)
    flux = hlle_flux(left, right, normal)
    return trimmed(flux, along, 1, 0) - trimmed(flux, along, 0, 1)


def tendency(padded):
    prims = primitive(padded)
    across_x = trimmed(divergence(prims, 1, 0), 2, 2, 2)
    across_y = trimmed(divergence(prims, 2, 1), 1, 2, 2)
    wrapped = jnp.concatenate([prims[..., -2:], prims, prims[..., :2]], axis=3)
    across_z = trimmed(trimmed(divergence(wrapped, 3, 2), 1, 2, 2), 2, 2, 2)
    return -(across_x + across_y + across_z)


def signal_speed(state):
    prims = primitive(state)
    fastest = jnp.abs(prims[1]) + fast_speed(prims, 0)
    fastest = jnp.maximum(fastest, jnp.abs(prims[2]) + fast_speed(prims, 1))
    return jnp.maximum(fastest, jnp.abs(prims[3]) + fast_speed(prims, 2))


def global_speed(local_top):
    return lax.pmax(local_top, ("group", "dev"))


def with_ghosts(slab):
    return with_halo(slab, (("group", 1), ("dev", 2)), 2)


def body(blocks_in, counts):
    fields = blocks_in.shape[1]
    cells = blocks_in.shape[2]
    own_count = counts[0]
    every_count = lax.all_gather(counts, ("group", "dev"), axis=0, tiled=True)
    position = lax.axis_index(("group", "dev"))
    earlier = jnp.arange(every_count.shape[0], dtype=jnp.int32) < position
    start_here = jnp.sum(jnp.where(earlier, every_count, 0))
    surplus = start_here - position * BLK_DEV
    padded_slots = jnp.concatenate(
        [jnp.zeros((BLK_DEV, fields, cells), jnp.float32), blocks_in], axis=0
    )
    outgoing = lax.dynamic_slice_in_dim(padded_slots, own_count, BLK_DEV, 0)
    incoming = passed_along(outgoing, ("group", "dev"), 1)
    joined = jnp.concatenate([incoming, blocks_in], axis=0)
    mine = lax.dynamic_slice_in_dim(joined, BLK_DEV - surplus, BLK_DEV, 0)
    slab = mine.reshape(BRICK_X, BRICK_Y, BRICK_Z, fields, BS, BS, BS)
    slab = jnp.transpose(slab, (3, 0, 4, 1, 5, 2, 6)).reshape(
        fields, BRICK_X * BS, BRICK_Y * BS, BRICK_Z * BS
    )
    speed = global_speed(jnp.max(signal_speed(slab)))
    step = COURANT / speed
    first = slab + step * tendency(with_ghosts(slab))
    second = 0.5 * (slab + first + step * tendency(with_ghosts(first)))
    result = second.reshape(fields, BRICK_X, BS, BRICK_Y, BS, BRICK_Z, BS)
    return jnp.transpose(result, (1, 3, 5, 0, 2, 4, 6)).reshape(BLK_DEV, fields, cells)


def solution(mesh):
    in_specs = (P(("group", "dev"), None, None), P(("group", "dev")))
    out_specs = P(("group", "dev"), None, None)
    return jax.shard_map(body, mesh=mesh, in_specs=in_specs, out_specs=out_specs, check_vma=False)
```

profile of v0, /device:TPU:1, one launch (start us, length us, event | category | flops | bytes accessed | tf_op | source)
XLA Modules:
  0.0 510.1 jit_solution(16989212895498887293)
XLA Ops:
  1.9 5.1 collective-permute-start
  7.1 57.7 %all-reduce.1 = s32[32]{0:T(128)S(1)} all-reduce(s32[32]{0:T(128)S(1)} %dynamic-update-slice), channel_id=1, replica_groups=mesh['group'=4,'dev'=8] {'group','dev'}, use_global_device_ids=true, to_apply=%add.1 | all-reduce | flops 32 | bytes 256
  68.0 9.0 %reshape.280 = f32[1,2,8,8,16,16,16]{6,5,4,3,2,1,0:T(8,128)} reshape(f32[16,8,4096]{2,1,0:T(8,128)S(1)} %fusion.37) | data formatting | bytes 4194304 | tf_op jit(solution)/shard_map/reshape | solution.py:172
  77.0 8.6 %fusion.155 = (f32[1,1,16,2,16,8,16]{6,4,2,0,5,3,1:T(8,128)S(1)}, f32[16,2,16,8,16]{4,2,0,3,1:T(8,128)}, f32[1,1,16,2,16,8,16]{6,4,2,0,5,3,1:T(8,128)}, f32[1,1,...) fusion(f32[8,1,16,2,16,8,16]{6,4,2,0,5,3,1:T(8,128)} %bitcast.526), kind=kLoop, calls=%fused_computation.450 | loop fusion | flops 262144 | bytes 2883584 | tf_op jit(solution)/shard_map/slice | solution.py:51
  85.6 17.9 %copy.31 = f32[8,1,16,2,16,8,16]{6,5,4,3,2,0,1:T(8,128)} copy(f32[8,1,16,2,16,8,16]{6,4,2,0,5,3,1:T(8,128)} %bitcast.527) | data formatting | bytes 4194304 | tf_op jit(solution)/shard_map/transpose | solution.py:173
  105.3 2.8 copy.39
  109.4 2.8 copy.38
  113.4 2.8 copy.37
  117.5 2.8 copy.33
  120.9 10.3 %multiply_reduce_fusion = (f32[16,2,16,8,16]{4,2,0,3,1:T(8,128)}, f32[16,2,16,8,16]{4,2,0,3,1:T(8,128)}, f32[3,1,16,2,16,8,16]{6,4,2,0,5,3,1:T(8,128)}) fusion(f32[16,2,16,8,16]{4,2,0,3,1:T(8,128)} %get-tuple-element.118, f32[8,1,16,2,16,8,16]{6,4,2,0,5,3,1:T(8,128)} %bitcast.528), kind=kLoop, calls=%fused_computation.40 | loop fusion | flops 851968 | bytes 3145728 | tf_op jit(solution)/shard_map/reduce_sum | solution.py:49
  131.2 10.7 %reshape.281 = f32[8,16,32,128]{3,2,1,0:T(8,128)S(1)} reshape(f32[8,1,16,2,16,8,16]{6,5,4,3,2,0,1:T(8,128)} %copy.31) | data formatting | bytes 4194304 | tf_op jit(solution)/shard_map/reshape | solution.py:173
  141.9 4.9 copy.35
  151.8 2.8 copy.36
  155.9 9.1 %copy.32 = f32[3,1,16,2,16,8,16]{6,5,4,3,2,0,1:T(8,128)} copy(f32[3,1,16,2,16,8,16]{6,4,2,0,5,3,1:T(8,128)} %get-tuple-element.123) | data formatting | bytes 1572864 | tf_op jit(solution)/shard_map/slice | solution.py:47
  164.9 4.3 slice.680
  172.0 4.0 collective-permute-start.3
  177.4 39.6 %pmax.7 = f32[]{:T(128)} all-reduce(f32[]{:T(128)} %fusion.122), channel_id=1, replica_groups=mesh['group'=4,'dev'=8] {'group','dev'}, use_global_device_ids=true, to_apply=%region_4.5 | all-reduce | flops 1 | bytes 8 | tf_op jit(solution)/shard_map/pmax | solution.py:149
  220.5 4.5 minimum_multiply_fusion.3
  226.1 9.8 %minimum_multiply_fusion.1 = f32[8,20,36,130]{3,2,1,0:T(8,128)} fusion(f32[8,20,36,2]{3,2,1,0:T(8,128)S(1)} %get-tuple-element.227, f32[3,20,36,128]{3,2,1,0:T(8,128)S(1)} %get-tuple-element.114, f32[1,20,36,128]{3,2,1,0:T(8,128)S(1)} %fusion.74, f32[3,20,36,128]{3,2,1,0:T(8,128)S(1)} %get-tuple-element.291, ...), kind=kLoop, calls=%fused_computation.37 | loop fusion | flops 17222400 | bytes 6036480 | tf_op jit(solution)/shard_map/mul | solution.py:119
  235.8 6.8 %pad_maximum_fusion.10 = (f32[8,20,36,130]{3,2,1,0:T(8,128)}, f32[8,20,36,130]{3,2,1,0:T(8,128)}) fusion(f32[8,20,36,2]{3,2,1,0:T(8,128)S(1)} %get-tuple-element.227, f32[3,20,36,128]{3,2,1,0:T(8,128)S(1)} %get-tuple-element.114, f32[1,20,36,128]{3,2,1,0:T(8,128)S(1)} %fusion.74, f32[3,20,36,128]{3,2,1,0:T(8,128)S(1)} %get-tuple-element.291, ...), kind=kLoop, calls=%fused_computation.18 | loop fusion | flops 5990400 | bytes 9031680 | tf_op jit(solution)/shard_map/concatenate | solution.py:136
  245.3 4.1 fusion.16
  258.5 3.4 fusion.31
  268.9 3.2 fusion.19
  272.1 3.1 fusion.160
  275.2 10.7 %fusion.3 = (f32[8,20,36,129]{3,2,1,0:T(8,128)S(1)}, f32[8,20,36,129]{3,2,1,0:T(8,128)S(1)}) fusion(f32[8,20,36,130]{3,2,1,0:T(8,128)} %minimum_multiply_fusion.1, f32[8,20,36,130]{3,2,1,0:T(8,128)} %get-tuple-element.224, f32[8,20,36,130]{3,2,1,0:T(8,128)} %get-tuple-element.225), kind=kLoop, calls=%fused_computation.12 | loop fusion | flops 2972160 | bytes 17832960 | tf_op jit(solution)/shard_map/sub | solution.py:127
  293.5 3.3 multiply_bitcast_fusion.1
  298.5 7.4 %multiply_add_fusion.2 = (f32[3,20,36,129]{3,2,1,0:T(8,128)}, f32[3,20,36,129]{3,2,1,0:T(8,128)}, f32[3,20,36,129]{3,2,1,0:T(8,128)}, f32[3,20,36,129]{3,2,1,0:T...) fusion(f32[20,36,129]{2,1,0:T(8,128)S(1)} %get-tuple-element.134, ...), kind=kLoop, calls=%fused_computation.117 | loop fusion | flops 5015520 | bytes 14117772 | tf_op jit(solution)/shard_map/add | solution.py:89
  305.9 9.1 %fusion.6 = f32[8,20,36,129]{3,2,1,0:T(8,128)S(1)} fusion(f32[3,20,36,129]{3,2,1,0:T(8,128)} %get-tuple-element.287, f32[1,20,36,129]{3,2,1,0:T(8,128)} %get-tuple-element.111, f32[3,20,36,129]{3,2,1,0:T(8,128)} %get-tuple-element.288, f32[1,20,36,129]{3,2,1,0:T(8,128)} %get-tuple-element.160, f32[3,20,36,129]{3,2,1,0:T(8,128)} %get-tuple-element.126, ...), kind=kLoop, calls=%fused_computation.23 | loop fusion | flops 14117760 | bytes 16346880 | tf_op jit(solution)/shard_map/div | solution.py:113
  318.2 3.8 fusion.47
  325.3 5.2 %collective-permute-done.5 = f32[8,2,32,128]{3,2,1,0:T(8,128)S(1)} collective-permute-done((f32[8,2,32,128]{3,2,1,0:T(8,128)S(1)}, f32[8,2,32,128]{3,2,1,0:T(8,128)S(1)}, u32[]{:S(2)}, u32[]{:S(2)}) %collective-permute-start.5) | collective-permute-done | bytes 262176 | tf_op jit(solution)/shard_map/ppermute | solution.py:26
  330.5 7.2 %collective-permute-done.6 = f32[8,2,32,128]{3,2,1,0:T(8,128)S(1)} collective-permute-done((f32[8,2,32,128]{3,2,1,0:T(8,128)S(1)}, f32[8,2,32,128]{3,2,1,0:T(8,128)S(1)}, u32[]{:S(2)}, u32[]{:S(2)}) %collective-permute-start.6) | collective-permute-done | bytes 262176 | tf_op jit(solution)/shard_map/ppermute | solution.py:28
  342.6 3.0 collective-permute-done.8
  348.3 4.5 minimum_multiply_fusion.2
  353.8 10.0 %minimum_multiply_fusion = f32[8,20,36,130]{3,2,1,0:T(8,128)} fusion(f32[8,20,36,2]{3,2,1,0:T(8,128)S(1)} %get-tuple-element.209, f32[3,20,36,128]{3,2,1,0:T(8,128)S(1)} %get-tuple-element.77, f32[1,20,36,128]{3,2,1,0:T(8,128)S(1)} %fusion.71, f32[3,20,36,128]{3,2,1,0:T(8,128)S(1)} %get-tuple-element.79, f32[1,20,36,128]{3,2,1,0:T(8,128)S(1)} %maximum_maximum_fusion.4, ...), kind=kLoop, calls=%fused_computation.36 | loop fusion | flops 17222400 | bytes 6036480 | tf_op jit(solution)/shard_map/mul | solution.py:119
  363.8 6.5 %pad_maximum_fusion.11 = (f32[8,20,36,130]{3,2,1,0:T(8,128)}, f32[8,20,36,130]{3,2,1,0:T(8,128)}) fusion(f32[8,20,36,2]{3,2,1,0:T(8,128)S(1)} %get-tuple-element.209, f32[3,20,36,128]{3,2,1,0:T(8,128)S(1)} %get-tuple-element.77, f32[1,20,36,128]{3,2,1,0:T(8,128)S(1)} %fusion.71, f32[3,20,36,128]{3,2,1,0:T(8,128)S(1)} %get-tuple-element.79, ...), kind=kLoop, calls=%fused_computation.27 | loop fusion | flops 5990400 | bytes 9031680 | tf_op jit(solution)/shard_map/concatenate | solution.py:136
  375.2 4.0 fusion.14
  388.0 3.9 multiply_add_fusion.8
  391.9 4.0 fusion.35
  406.1 4.1 fusion.23
  410.2 3.1 fusion.158
  413.3 13.2 %fusion.1 = (f32[8,20,36,129]{3,2,1,0:T(8,128)S(1)}, f32[8,20,36,129]{3,2,1,0:T(8,128)}) fusion(f32[8,20,36,130]{3,2,1,0:T(8,128)} %minimum_multiply_fusion, f32[8,20,36,130]{3,2,1,0:T(8,128)} %get-tuple-element.206, f32[8,20,36,130]{3,2,1,0:T(8,128)} %get-tuple-element.207), kind=kLoop, calls=%fused_computation.3 | loop fusion | flops 2972160 | bytes 17832960 | tf_op jit(solution)/shard_map/sub | solution.py:127
  435.9 4.9 multiply_bitcast_fusion
  441.9 8.0 %multiply_add_fusion = (f32[3,20,36,129]{3,2,1,0:T(8,128)}, f32[3,20,36,129]{3,2,1,0:T(8,128)}, f32[3,20,36,129]{3,2,1,0:T(8,128)}, f32[3,20,36,129]{3,2,1,0:T(8...) fusion(f32[20,36,129]{2,1,0:T(8,128)} %get-tuple-element.130, f32[20,36,129]{2,1,0:T(8,128)} %get-tuple-element.147, ...), kind=kLoop, calls=%fused_computation.107 | loop fusion | flops 5015520 | bytes 14117772 | tf_op jit(solution)/shard_map/add | solution.py:89
  449.9 9.5 %fusion.10 = f32[8,20,36,129]{3,2,1,0:T(8,128)S(1)} fusion(f32[3,20,36,129]{3,2,1,0:T(8,128)} %get-tuple-element.278, f32[1,20,36,129]{3,2,1,0:T(8,128)} %get-tuple-element.74, f32[3,20,36,129]{3,2,1,0:T(8,128)} %get-tuple-element.279, f32[1,20,36,129]{3,2,1,0:T(8,128)} %get-tuple-element.142, f32[3,20,36,129]{3,2,1,0:T(8,128)} %get-tuple-element.124, ...), kind=kLoop, calls=%fused_computation.32 | loop fusion | flops 14117760 | bytes 16346880 | tf_op jit(solution)/shard_map/div | solution.py:113
  462.2 7.4 %fusion.42 = f32[8,16,32,128]{3,2,1,0:T(8,128)} fusion(f32[8,20,36,128]{3,2,1,0:T(8,128)} %get-tuple-element.139, f32[8,20,36,128]{3,2,1,0:T(8,128)S(1)} %get-tuple-element.138, f32[8,20,32,128]{3,2,1,0:T(8,128)} %get-tuple-element.193, f32[8,20,32,128]{3,2,1,0:T(8,128)} %get-tuple-element.192, f32[8,16,36,128]{3,2,1,0:T(8,128)} %get-tuple-element.237, ...), kind=kLoop, calls=%fused_computation.130 | loop fusion | flops 5242880 | bytes 18874372 | tf_op jit(solution)/shard_map/mul | solution.py:179
  469.6 10.6 %reshape.282 = f32[8,1,16,2,16,8,16]{6,5,4,3,2,0,1:T(8,128)} reshape(f32[8,16,32,128]{3,2,1,0:T(8,128)} %fusion.42) | data formatting | bytes 4194304 | tf_op jit(solution)/shard_map/reshape | solution.py:180
  480.2 14.1 %copy.40 = f32[1,2,8,8,16,16,16]{6,5,4,3,2,1,0:T(8,128)} copy(f32[1,2,8,8,16,16,16]{6,2,5,1,4,3,0:T(8,128)} %bitcast.529) | data formatting | bytes 4194304 | tf_op jit(solution)/shard_map/transpose | solution.py:181
  494.3 15.2 %reshape.283 = f32[16,8,4096]{2,1,0:T(8,128)} reshape(f32[1,2,8,8,16,16,16]{6,5,4,3,2,1,0:T(8,128)} %copy.40) | data formatting | bytes 4194304 | tf_op jit(solution)/shard_map/reshape | solution.py:181
  (165 shorter events, 104.0 us)
Async XLA Ops:
  1.9 64.2 %collective-permute-start = (f32[16,8,4096]{2,1,0:T(8,128)S(1)}, f32[16,8,4096]{2,1,0:T(8,128)}, u32[]{:S(2)}, u32[]{:S(2)}) collective-permute-start(f32[16,8,4096]{2,1,0:T(8,128)S(1)} %pad_dynamic-slice_fusion.2), channel_id=1, source_target_pairs={{0,1},{1,2},{2,3},{3,4},{4,5},{5,6},{6,7},{7,8},{8,9},{9,10},{10,1... | collective-permute-start | bytes 6291464 | tf_op jit(solution)/shard_map/ppermute | solution.py:38
  141.9 7.7 %copy-start.1 = (f32[8,16,32,128]{3,2,1,0:T(8,128)}, f32[8,16,32,128]{3,2,1,0:T(8,128)S(1)}, u32[]{:S(2)}) copy-start(f32[8,16,32,128]{3,2,1,0:T(8,128)S(1)} %reshape.281) | copy-start | bytes 6291460
  150.3 20.8 %collective-permute-start.2 = (f32[8,2,32,128]{3,2,1,0:T(8,128)}, f32[8,2,32,128]{3,2,1,0:T(8,128)S(1)}, u32[]{:S(2)}, u32[]{:S(2)}) collective-permute-start(f32[8,2,32,128]{3,2,1,0:T(8,128)} %get-tuple-element.270), channel_id=1, source_target_pairs={{8,0},{16,8},{24,16},{0,24},{9,1},{17,9},{25,17},{1,25},{10,2},{18... | collective-permute-start | bytes 786440 | tf_op jit(solution)/shard_map/ppermute | solution.py:28
  151.6 17.8 %collective-permute-start.1 = (f32[8,2,32,128]{3,2,1,0:T(8,128)S(1)}, f32[8,2,32,128]{3,2,1,0:T(8,128)}, u32[]{:S(2)}, u32[]{:S(2)}) collective-permute-start(f32[8,2,32,128]{3,2,1,0:T(8,128)S(1)} %get-tuple-element.271), channel_id=1, source_target_pairs={{0,8},{8,16},{16,24},{24,0},{1,9},{9,17},{17,25},{25,1},{2,10},{10... | collective-permute-start | bytes 786440 | tf_op jit(solution)/shard_map/ppermute | solution.py:26
  169.3 1.7 copy-start.2
  169.4 6.6 %copy-start.27 = (f32[16,32,128]{2,1,0:T(8,128)S(1)}, f32[16,32,128]{2,1,0:T(8,128)}, u32[]{:S(2)}) copy-start(f32[16,32,128]{2,1,0:T(8,128)} %mul.2246) | copy-start | bytes 786436
  169.4 6.6 %copy-start.28 = (f32[16,32,128]{2,1,0:T(8,128)S(1)}, f32[16,32,128]{2,1,0:T(8,128)}, u32[]{:S(2)}) copy-start(f32[16,32,128]{2,1,0:T(8,128)} %mul.2242) | copy-start | bytes 786436
  169.4 6.6 %copy-start.29 = (f32[16,32,128]{2,1,0:T(8,128)S(1)}, f32[16,32,128]{2,1,0:T(8,128)}, u32[]{:S(2)}) copy-start(f32[16,32,128]{2,1,0:T(8,128)} %mul.2238) | copy-start | bytes 786436
  169.4 6.6 %copy-start.30 = (f32[16,32,128]{2,1,0:T(8,128)S(1)}, f32[16,32,128]{2,1,0:T(8,128)}, u32[]{:S(2)}) copy-start(f32[16,32,128]{2,1,0:T(8,128)} %reduce_sum.577) | copy-start | bytes 786436
  169.4 6.6 %copy-start.31 = (f32[16,32,128]{2,1,0:T(8,128)S(1)}, f32[16,32,128]{2,1,0:T(8,128)}, u32[]{:S(2)}) copy-start(f32[16,32,128]{2,1,0:T(8,128)} %reduce_sum.579) | copy-start | bytes 786436
  172.0 45.8 %collective-permute-start.3 = (f32[8,20,2,128]{3,2,1,0:T(2,128)}, f32[8,20,2,128]{3,2,1,0:T(2,128)S(1)}, u32[]{:S(2)}, u32[]{:S(2)}) collective-permute-start(f32[8,20,2,128]{3,2,1,0:T(2,128)} %get-tuple-element.266), channel_id=1, source_target_pairs={{0,1},{1,2},{2,3},{3,4},{4,5},{5,6},{6,7},{7,0},{8,9},{9,10},{10,1... | collective-permute-start | bytes 491528 | tf_op jit(solution)/shard_map/ppermute | solution.py:26
  176.0 41.8 %collective-permute-start.4 = (f32[8,20,2,128]{3,2,1,0:T(2,128)}, f32[8,20,2,128]{3,2,1,0:T(2,128)S(1)}, u32[]{:S(2)}, u32[]{:S(2)}) collective-permute-start(f32[8,20,2,128]{3,2,1,0:T(2,128)} %get-tuple-element.267), channel_id=1, source_target_pairs={{1,0},{2,1},{3,2},{4,3},{5,4},{6,5},{7,6},{0,7},{9,8},{10,9},{11,1... | collective-permute-start | bytes 491528 | tf_op jit(solution)/shard_map/ppermute | solution.py:28
  249.8 1.0 copy-start.21
  249.9 1.1 copy-start.22
  249.9 1.2 copy-start.23
  250.2 2.0 copy-start.17
  250.3 2.0 copy-start.18
  253.4 2.6 copy-start.34
  256.0 2.5 copy-start.16
  265.8 2.3 copy-start.32
  293.5 4.4 copy-start.33
  296.8 1.4 copy-start.10
  296.8 1.7 copy-start.11
  315.0 1.6 copy-start.3
  315.0 2.4 copy-start.6
  315.0 3.2 copy-start.7
  322.0 8.5 %collective-permute-start.5 = (f32[8,2,32,128]{3,2,1,0:T(8,128)S(1)}, f32[8,2,32,128]{3,2,1,0:T(8,128)S(1)}, u32[]{:S(2)}, u32[]{:S(2)}) collective-permute-start(f32[8,2,32,128]{3,2,1,0:T(8,128)S(1)} %get-tuple-element.268), channel_id=1, source_target_pairs={{0,8},{8,16},{16,24},{24,0},{1,9},{9,17},{17,25},{25,1},{2,10},{10... | collective-permute-start | bytes 786440 | tf_op jit(solution)/shard_map/ppermute | solution.py:26
  323.9 13.7 %collective-permute-start.6 = (f32[8,2,32,128]{3,2,1,0:T(8,128)S(1)}, f32[8,2,32,128]{3,2,1,0:T(8,128)S(1)}, u32[]{:S(2)}, u32[]{:S(2)}) collective-permute-start(f32[8,2,32,128]{3,2,1,0:T(8,128)S(1)} %get-tuple-element.269), channel_id=1, source_target_pairs={{8,0},{16,8},{24,16},{0,24},{9,1},{17,9},{25,17},{1,25},{10,2},{18... | collective-permute-start | bytes 786440 | tf_op jit(solution)/shard_map/ppermute | solution.py:28
  337.8 4.8 collective-permute-start.7
  340.0 5.6 %collective-permute-start.8 = (f32[8,20,2,128]{3,2,1,0:T(2,128)S(1)}, f32[8,20,2,128]{3,2,1,0:T(2,128)S(1)}, u32[]{:S(2)}, u32[]{:S(2)}) collective-permute-start(f32[8,20,2,128]{3,2,1,0:T(2,128)S(1)} %get-tuple-element.265), channel_id=1, source_target_pairs={{1,0},{2,1},{3,2},{4,3},{5,4},{6,5},{7,6},{0,7},{9,8},{10,9},{11,1... | collective-permute-start | bytes 491528 | tf_op jit(solution)/shard_map/ppermute | solution.py:28
  370.7 2.4 copy-start.4
  380.7 1.9 copy-start.5
  380.7 2.0 copy-start.24
  380.7 2.1 copy-start.25
  380.7 2.2 copy-start.26
  381.8 2.2 copy-start.19
  381.8 2.2 copy-start.20
  385.1 2.8 copy-start.35
  388.0 3.9 copy-start.8
  388.0 3.9 copy-start.9
  396.0 2.8 copy-start.13
  396.0 2.8 copy-start.14
  396.0 2.8 copy-start.15
  398.7 1.4 copy-start.12
  426.5 2.9 copy-start
where the time goes:
time: 517 us; the launch traced here: 510 us
  other arithmetic  226 us (44%)
  local copies, waits for them, and re-layouts  149 us (29%)
  blocking collectives  97.3 us (19%)
  waiting for transfers between devices  17.8 us (3%)
  starting transfers between devices  16.2 us (3%)
    unnamed x1, blocking collectives  57.7 us
    pmax x1, blocking collectives, global_speed(): return lax.pmax(local_top, ('group', 'dev'))  39.6 us
    div x12, other arithmetic, hlle_flux(): (upper * flux_left - lower * flux_right + upper * lower * (state_right -...  38.5 us
    sub x6, other arithmetic, divergence(): right = trimmed(prims, along, 2, 1) - 0.5 * trimmed(slope, along, 1, 0)  32.8 us
    mul x6, other arithmetic, minmod(): 0.5 * (jnp.sign(first) + jnp.sign(second))  31.3 us
    add x6, other arithmetic, physical_flux(): density * velocity * speed_normal - magnetic * field_normal  25 us
    transpose x1, local copies, waits for them, and re-layouts, body(): jnp.transpose(slab, (3, 0, 4, 1, 5, 2, 6))  17.9 us
    sub x12, other arithmetic, physical_flux(): (state[4] + total_pressure) * speed_normal  17.4 us
  transfers between devices with their start and end apart: 9, of which 4 were waited for; matrix products, arithmetic and copies ran while one was open for 4% of the time, Pallas kernels for 0%

commit v1 on v0

v1 whole, which is shorter than its diff:
```python
import functools

import jax
import jax.numpy as jnp
from jax import lax
from jax.experimental import pallas as pl
from jax.experimental.pallas import tpu as pltpu
from jax.sharding import PartitionSpec as P

BS = 16
BRICK_Y = 2
BRICK_Z = 8
BLK_DEV = 16
FIELDS = 8
LANES = 128
CHUNKS = 32
ROWS = CHUNKS * FIELDS
YV = 4

GAMMA = 5.0 / 3.0
COURANT = 0.25
DENSITY_FLOOR = 0.05
PRESSURE_FLOOR = 0.05
TINY = 1.2e-38

MESH = pl.DeviceIdType.MESH


def primitive(u):
    density = jnp.maximum(u[0], DENSITY_FLOOR)
    inverse = 1.0 / density
    vx, vy, vz = u[1] * inverse, u[2] * inverse, u[3] * inverse
    kinetic = 0.5 * density * (vx * vx + vy * vy + vz * vz)
    energy_b = 0.5 * (u[5] * u[5] + u[6] * u[6] + u[7] * u[7])
    pressure = jnp.maximum((GAMMA - 1.0) * (u[4] - kinetic - energy_b), PRESSURE_FLOOR)
    return [density, vx, vy, vz, pressure, u[5], u[6], u[7]], inverse


def fast_from(sound, alfven, along):
    total = sound + alfven
    inner = jnp.maximum(total * total - 4.0 * sound * along, TINY)
    outer = 0.5 * (total + inner * lax.rsqrt(inner))
    return outer * lax.rsqrt(outer)


def side(w, n):
    r, v, p, b = w[0], w[1:4], w[4], w[5:8]
    inverse = 1.0 / r
    b2 = b[0] * b[0] + b[1] * b[1] + b[2] * b[2]
    v2 = v[0] * v[0] + v[1] * v[1] + v[2] * v[2]
    half_b2 = 0.5 * b2
    m = [r * v[0], r * v[1], r * v[2]]
    energy = p * (1.0 / (GAMMA - 1.0)) + 0.5 * r * v2 + half_b2
    total_p = p + half_b2
    vn, bn = v[n], b[n]
    fast = fast_from(GAMMA * p * inverse, b2 * inverse, bn * bn * inverse)
    vb = v[0] * b[0] + v[1] * b[1] + v[2] * b[2]
    fm = [m[i] * vn - b[i] * bn for i in range(3)]
    fm[n] = fm[n] + total_p
    fe = (energy + total_p) * vn - bn * vb
    fb = [None if i == n else vn * b[i] - v[i] * bn for i in range(3)]
    return [r] + m + [energy] + b, [m[n]] + fm + [fe] + fb, vn, fast


def hlle(left, right, n):
    ul, fl, vl, cl = side(left, n)
    ur, fr, vr, cr = side(right, n)
    upper = jnp.maximum(jnp.maximum(vr + cr, vl + cl), 0.0)
    lower = jnp.minimum(jnp.minimum(vl - cl, vr - cr), 0.0)
    inverse = 1.0 / (upper - lower)
    a = upper * inverse
    b = lower * inverse
    c = a * lower
    out = []
    for f in range(FIELDS):
        jump = c * (ur[f] - ul[f])
        out.append(jump if fl[f] is None else a * fl[f] - b * fr[f] + jump)
    return out


def half_minmod(a, b):
    return 0.5 * (jnp.maximum(jnp.minimum(a, b), 0.0) + jnp.minimum(jnp.maximum(a, b), 0.0))


def roll(x, shift, axis):
    size = x.shape[axis]
    shift = shift % size
    return x if shift == 0 else pltpu.roll(x, shift, axis)


def lane_index():
    return lax.broadcasted_iota(jnp.int32, (8, LANES), 1)


def z_up(x, last):
    return jnp.where(last, roll(roll(x, 15, 1), -1, 0), roll(x, -1, 1))


def z_down(x, first):
    return jnp.where(first, roll(roll(x, -15, 1), 1, 0), roll(x, 1, 1))


def fill_primitives(u_ref, xlo_ref, xhi_ref, glo_ref, ghi_ref, w_ref):
    def planes(source, base):
        def one(c, carry):
            for v in range(YV):
                w, _ = primitive([source[c, f, v] for f in range(FIELDS)])
                for f in range(FIELDS):
                    w_ref[base + c, f, v + 1] = w[f]
            return carry

        lax.fori_loop(0, source.shape[0], one, 0)

    planes(xlo_ref, 0)
    planes(u_ref, 2)
    planes(xhi_ref, 2 + BS)

    def ghosts(c, carry):
        for ghost, v, base in ((glo_ref, 0, 96), (ghi_ref, YV + 1, 0)):
            u = [roll(ghost[c, f // 4], base - 32 * (f % 4), 1) for f in range(FIELDS)]
            w, _ = primitive(u)
            for f in range(FIELDS):
                w_ref[c + 2, f, v] = w[f]
        return carry

    lax.fori_loop(0, BS, ghosts, 0)


def x_faces(w_ref, fx_ref):
    for v in range(YV):
        def one(face, slope):
            left, right, after = [], [], []
            for f in range(FIELDS):
                here = w_ref[face + 1, f, v + 1]
                there = w_ref[face + 2, f, v + 1]
                beyond = w_ref[face + 3, f, v + 1]
                new = half_minmod(there - here, beyond - there)
                left.append(here + slope[f])
                right.append(there - new)
                after.append(new)
            flux = hlle(left, right, 0)
            for f in range(FIELDS):
                fx_ref[face, f, v] = flux[f]
            return tuple(after)

        first = tuple(
            half_minmod(
                w_ref[1, f, v + 1] - w_ref[0, f, v + 1], w_ref[2, f, v + 1] - w_ref[1, f, v + 1]
            )
            for f in range(FIELDS)
        )
        lax.fori_loop(0, BS + 1, one, first)


def y_faces(w_ref, c, f_ref):
    lane = lane_index()
    top = lane >= LANES - BS
    bottom = lane < BS
    left = [[None] * FIELDS for _ in range(YV + 1)]
    right = [[None] * FIELDS for _ in range(YV + 1)]
    for f in range(FIELDS):
        w = [w_ref[c + 2, f, v] for v in range(YV + 2)]
        rolled = [roll(x, -BS, 1) for x in w]
        up = [jnp.where(top, rolled[min(v + 1, YV + 1)], rolled[v]) for v in range(YV + 2)]
        diff = [up[v] - w[v] for v in range(YV + 2)]
        rolled = [roll(x, BS, 1) for x in diff]
        down = [jnp.where(bottom, rolled[max(v - 1, 0)], rolled[v]) for v in range(YV + 2)]
        slope = [half_minmod(down[v], diff[v]) for v in range(YV + 2)]
        low = [roll(w[v] - slope[v], -BS, 1) for v in range(YV + 2)]
        for v in range(YV + 1):
            left[v][f] = w[v] + slope[v]
            right[v][f] = jnp.where(top, low[v + 1], low[v])
    for v in range(YV + 1):
        flux = hlle(left[v], right[v], 1)
        for f in range(FIELDS):
            f_ref[f, v] = flux[f]


def tile_tendency(w_ref, fx_ref, fy_ref, c, v):
    lane = lane_index()
    bottom = lane < BS
    cz = lane % BS
    last, start = cz == BS - 1, cz == 0
    left, right = [], []
    for f in range(FIELDS):
        w = w_ref[c + 2, f, v + 1]
        diff = z_up(w, last) - w
        slope = half_minmod(z_down(diff, start), diff)
        left.append(w + slope)
        right.append(z_up(w - slope, last))
    flux = hlle(left, right, 2)
    out = []
    for f in range(FIELDS):
        across_z = flux[f] - z_down(flux[f], start)
        upper = fy_ref[f, v + 1]
        across_y = upper - jnp.where(bottom, roll(fy_ref[f, v], BS, 1), roll(upper, BS, 1))
        across_x = fx_ref[c + 1, f, v] - fx_ref[c, f, v]
        out.append(across_x + across_y + across_z)
    return out


def pack(tiles, base):
    group = lane_index() // 32
    out = []
    for q in range(2):
        total = roll(tiles[4 * q], -base, 1)
        for k in range(1, 4):
            total = jnp.where(group == k, roll(tiles[4 * q + k], 32 * k - base, 1), total)
        out.append(total)
    return out


def first_kernel(step_ref, u_ref, xlo, xhi, glo, ghi, out_ref, plo_ref, phi_ref, w_ref, fx_ref, fy_ref):
    fill_primitives(u_ref, xlo, xhi, glo, ghi, w_ref)
    x_faces(w_ref, fx_ref)

    def one(c, carry):
        step = step_ref[...]
        y_faces(w_ref, c, fy_ref)
        for v in range(YV):
            change = tile_tendency(w_ref, fx_ref, fy_ref, c, v)
            new = [u_ref[c, f, v] - step * change[f] for f in range(FIELDS)]
            for f in range(FIELDS):
                out_ref[c, f, v] = new[f]
            if v == 0:
                for q, tile in enumerate(pack(new, 0)):
                    plo_ref[c, q] = tile
            if v == YV - 1:
                for q, tile in enumerate(pack(new, 96)):
                    phi_ref[c, q] = tile
        return carry

    lax.fori_loop(0, BS, one, 0)


def second_kernel(step_ref, u_ref, one_ref, xlo, xhi, glo, ghi, out_ref, w_ref, fx_ref, fy_ref):
    fill_primitives(one_ref, xlo, xhi, glo, ghi, w_ref)
    x_faces(w_ref, fx_ref)

    def one(c, carry):
        step = step_ref[...]
        y_faces(w_ref, c, fy_ref)
        for v in range(YV):
            change = tile_tendency(w_ref, fx_ref, fy_ref, c, v)
            for f in range(FIELDS):
                new = 0.5 * (u_ref[c, f, v] + one_ref[c, f, v] - step * change[f])
                row = (v // 2) * (BRICK_Z * ROWS) + (c * 2 + v % 2) * FIELDS + f
                out_ref[pl.ds(row, BRICK_Z, stride=ROWS), :] = new
        return carry

    lax.fori_loop(0, BS, one, 0)


def ring(groups, devs):
    g, j = lax.axis_index("group"), lax.axis_index("dev")
    me = g * devs + j
    count = groups * devs
    after, before = lax.rem(me + 1, count), lax.rem(me + count - 1, count)
    curve_next = (after // devs, lax.rem(after, devs))
    curve_prev = (before // devs, lax.rem(before, devs))
    row = [(g, lax.rem(j + d, devs)) for d in range(1, devs)]
    column = [(lax.rem(g + d, groups), j) for d in range(1, groups)]
    return g, j, me, curve_next, curve_prev, row, column


def greet(peers):
    barrier = pltpu.get_barrier_semaphore()
    for peer in peers:
        pl.semaphore_signal(barrier, inc=1, device_id=peer, device_id_type=MESH)
    pl.semaphore_wait(barrier, len(peers))


def remote(source, target, send, recv, device):
    return pltpu.make_async_remote_copy(
        src_ref=source, dst_ref=target, send_sem=send, recv_sem=recv,
        device_id=device, device_id_type=MESH,
    )


def spread(source, slots, send, recv, peers):
    copies = [remote(source, slots.at[d], send.at[d], recv.at[d], p) for d, p in enumerate(peers)]
    for copy in copies:
        copy.start()
    for copy in copies:
        copy.wait()


def halo(g, j, groups, devs, u_ref, plo_ref, phi_ref, xlo, xhi, glo, ghi, send, recv):
    up = (lax.rem(g + 1, groups), j)
    down = (lax.rem(g + groups - 1, groups), j)
    right = (g, lax.rem(j + 1, devs))
    left = (g, lax.rem(j + devs - 1, devs))
    copies = [
        remote(u_ref.at[pl.ds(BS - 2, 2)], xlo, send.at[0], recv.at[0], up),
        remote(u_ref.at[pl.ds(0, 2)], xhi, send.at[1], recv.at[1], down),
        remote(phi_ref, glo, send.at[2], recv.at[2], right),
        remote(plo_ref, ghi, send.at[3], recv.at[3], left),
    ]
    for copy in copies:
        copy.start()
    for copy in copies:
        copy.wait()


def halo_kernel(groups, devs, u_ref, plo_ref, phi_ref, xlo, xhi, glo, ghi, send, recv):
    g, j = lax.axis_index("group"), lax.axis_index("dev")
    greet([
        (lax.rem(g + 1, groups), j),
        (lax.rem(g + groups - 1, groups), j),
        (g, lax.rem(j + 1, devs)),
        (g, lax.rem(j + devs - 1, devs)),
    ])
    halo(g, j, groups, devs, u_ref, plo_ref, phi_ref, xlo, xhi, glo, ghi, send, recv)


def signal_speed(u):
    w, inverse = primitive(u)
    b2 = [w[5 + i] * w[5 + i] for i in range(3)]
    sound = GAMMA * w[4] * inverse
    alfven = (b2[0] + b2[1] + b2[2]) * inverse
    speeds = [jnp.abs(w[1 + i]) + fast_from(sound, alfven, b2[i] * inverse) for i in range(3)]
    return jnp.maximum(jnp.maximum(speeds[0], speeds[1]), speeds[2])


def stage_kernel(count_ref, own_ref, out_ref, sem):
    copies = []
    for m in range(BLK_DEV - 1):
        base = jnp.maximum(count_ref[0] - BLK_DEV + 1 + m, 0) * ROWS
        copies.append(pltpu.make_async_copy(
            own_ref.at[pl.ds(pl.multiple_of(base, ROWS), ROWS)],
            out_ref.at[pl.ds(m * ROWS, ROWS)],
            sem.at[m],
        ))
    for copy in copies:
        copy.start()
    for copy in copies:
        copy.wait()


def gather_kernel(
    groups, devs, cap, count_ref, outgoing, own_ref,
    step_ref, small_ref, joined,
    count_msg, count_row, count_col, speed_msg, speed_row, speed_col,
    total_ref, block_sem, row_send, row_recv, col_send, col_recv,
    srow_send, srow_recv, scol_send, scol_recv, local_sem,
):
    g, j, me, curve_next, curve_prev, row, column = ring(groups, devs)
    greet(row + column + [curve_next, curve_prev])
    count = count_ref[0]
    blocks = remote(
        outgoing, joined.at[pl.ds(ROWS, (BLK_DEV - 1) * ROWS)], block_sem.at[0], block_sem.at[1],
        curve_next,
    )
    blocks.start()
    local = pltpu.make_async_copy(
        own_ref.at[pl.ds(0, BLK_DEV * ROWS)], joined.at[pl.ds(BLK_DEV * ROWS, BLK_DEV * ROWS)],
        local_sem.at[0],
    )
    local.start()

    count_msg[...] = jnp.full((8, LANES), count, jnp.int32)
    spread(count_msg, count_row, row_send, row_recv, row)
    before = jnp.zeros((8, LANES), jnp.int32)
    every = count_msg[...]
    for d in range(1, devs):
        value = count_row[d - 1]
        every = every + value
        before = before + jnp.where(d <= j, value, 0)
    count_msg[...] = every
    spread(count_msg, count_col, col_send, col_recv, column)
    for d in range(1, groups):
        before = before + jnp.where(d <= g, count_col[d - 1], 0)
    total_ref[...] = before - me * BLK_DEV
    narrow = pltpu.make_async_copy(total_ref, small_ref, local_sem.at[1])
    narrow.start()

    slot = lax.broadcasted_iota(jnp.int32, (8, LANES), 0)

    def chunk(t, top):
        for first in list(range(0, cap - 8, 8)) + [cap - 8]:
            u = [
                own_ref[pl.ds(first * ROWS + t * FIELDS + f, 8, stride=ROWS), :]
                for f in range(FIELDS)
            ]
            top = jnp.maximum(top, jnp.where(slot + first < count, signal_speed(u), 0.0))
        return top

    top = lax.fori_loop(0, CHUNKS, chunk, jnp.zeros((8, LANES), jnp.float32))
    speed_msg[...] = top
    spread(speed_msg, speed_row, srow_send, srow_recv, row)
    for d in range(devs - 1):
        top = jnp.maximum(top, speed_row[d])
    speed_msg[...] = top
    spread(speed_msg, speed_col, scol_send, scol_recv, column)
    for d in range(groups - 1):
        top = jnp.maximum(top, speed_col[d])
    top = jnp.max(jnp.max(top, axis=1, keepdims=True), axis=0, keepdims=True)
    step_ref[...] = COURANT / jnp.broadcast_to(top, (8, LANES))

    narrow.wait()
    local.wait()
    blocks.wait()


def assemble_kernel(small_ref, joined, u_ref, plo, phi):
    surplus = small_ref[0, 0]

    def assemble(c, carry):
        for v in range(YV):
            for f in range(FIELDS):
                base = (BLK_DEV - surplus + (v // 2) * BRICK_Z) * ROWS
                u_ref[c, f, v] = joined[
                    pl.ds(base + (c * 2 + v % 2) * FIELDS + f, BRICK_Z, stride=ROWS), :
                ]
        for q, tile in enumerate(pack([u_ref[c, f, 0] for f in range(FIELDS)], 0)):
            plo[c, q] = tile
        for q, tile in enumerate(pack([u_ref[c, f, YV - 1] for f in range(FIELDS)], 96)):
            phi[c, q] = tile
        return carry

    lax.fori_loop(0, BS, assemble, 0)


TILE = (8, LANES)
SLAB = (BS, FIELDS, YV) + TILE
EDGE = (2, FIELDS, YV) + TILE
PACK = (BS, 2) + TILE
LIMIT = 48 * 1024 * 1024


def f32(*shape):
    return jax.ShapeDtypeStruct(shape, jnp.float32)


VMEM = pl.BlockSpec(memory_space=pltpu.VMEM)
ANY = pl.BlockSpec(memory_space=pl.ANY)
SMEM = pl.BlockSpec(memory_space=pltpu.SMEM)


def body(groups, devs, blocks_in, counts):
    cap = blocks_in.shape[0]
    rows = blocks_in.reshape(cap, FIELDS, CHUNKS, LANES).transpose(0, 2, 1, 3)
    rows = rows.reshape(cap * ROWS, LANES)
    ghosts = (f32(*EDGE), f32(*EDGE), f32(*PACK), f32(*PACK))
    dma = pltpu.SemaphoreType.DMA
    plain = pltpu.CompilerParams(vmem_limit_bytes=LIMIT)
    outgoing = pl.pallas_call(
        stage_kernel,
        out_shape=f32((BLK_DEV - 1) * ROWS, LANES),
        in_specs=[SMEM, ANY],
        out_specs=VMEM,
        scratch_shapes=[dma((BLK_DEV - 1,))],
        compiler_params=plain,
        name="stage",
    )(counts, rows)
    step, small, joined = pl.pallas_call(
        functools.partial(gather_kernel, groups, devs, cap),
        out_shape=(
            f32(*TILE), jax.ShapeDtypeStruct(TILE, jnp.int32), f32(2 * BLK_DEV * ROWS, LANES)
        ),
        in_specs=[SMEM, VMEM, VMEM],
        out_specs=(VMEM, SMEM, VMEM),
        scratch_shapes=[
            pltpu.VMEM(TILE, jnp.int32),
            pltpu.VMEM((devs - 1,) + TILE, jnp.int32),
            pltpu.VMEM((groups - 1,) + TILE, jnp.int32),
            pltpu.VMEM(TILE, jnp.float32),
            pltpu.VMEM((devs - 1,) + TILE, jnp.float32),
            pltpu.VMEM((groups - 1,) + TILE, jnp.float32),
            pltpu.VMEM(TILE, jnp.int32),
            dma((2,)),
            dma((devs - 1,)), dma((devs - 1,)), dma((groups - 1,)), dma((groups - 1,)),
            dma((devs - 1,)), dma((devs - 1,)), dma((groups - 1,)), dma((groups - 1,)),
            dma((2,)),
        ],
        compiler_params=pltpu.CompilerParams(
            collective_id=0, has_side_effects=True, vmem_limit_bytes=LIMIT
        ),
        name="gather",
    )(counts, outgoing, rows)
    u, plo, phi = pl.pallas_call(
        assemble_kernel,
        out_shape=(f32(*SLAB), f32(*PACK), f32(*PACK)),
        in_specs=[SMEM, VMEM],
        out_specs=(VMEM,) * 3,
        compiler_params=plain,
        name="assemble",
    )(small, joined)

    def exchange(u, plo, phi, collective_id):
        return pl.pallas_call(
            functools.partial(halo_kernel, groups, devs),
            out_shape=ghosts,
            in_specs=[VMEM] * 3,
            out_specs=(VMEM,) * 4,
            scratch_shapes=[dma((4,)), dma((4,))],
            compiler_params=pltpu.CompilerParams(
                collective_id=collective_id, has_side_effects=True, vmem_limit_bytes=LIMIT
            ),
            name="halo",
        )(u, plo, phi)

    xlo, xhi, glo, ghi = exchange(u, plo, phi, 1)
    work = [
        pltpu.VMEM((BS + 4, FIELDS, YV + 2) + TILE, jnp.float32),
        pltpu.VMEM((BS + 1, FIELDS, YV) + TILE, jnp.float32),
        pltpu.VMEM((FIELDS, YV + 1) + TILE, jnp.float32),
    ]
    one, plo, phi = pl.pallas_call(
        first_kernel,
        out_shape=(f32(*SLAB), f32(*PACK), f32(*PACK)),
        in_specs=[VMEM] * 6,
        out_specs=(VMEM,) * 3,
        scratch_shapes=work,
        compiler_params=plain,
        name="first_stage",
    )(step, u, xlo, xhi, glo, ghi)

    xlo, xhi, glo, ghi = exchange(one, plo, phi, 2)
    out = pl.pallas_call(
        second_kernel,
        out_shape=f32(BLK_DEV * ROWS, LANES),
        in_specs=[VMEM] * 7,
        out_specs=VMEM,
        scratch_shapes=work,
        compiler_params=plain,
        name="second_stage",
    )(step, u, one, xlo, xhi, glo, ghi)
    out = out.reshape(BLK_DEV, CHUNKS, FIELDS, LANES).transpose(0, 2, 1, 3)
    return out.reshape(BLK_DEV, FIELDS, CHUNKS * LANES)


def solution(mesh):
    groups, devs = mesh.shape["group"], mesh.shape["dev"]
    in_specs = (P(("group", "dev"), None, None), P(("group", "dev")))
    out_specs = P(("group", "dev"), None, None)
    return jax.shard_map(
        functools.partial(body, groups, devs),
        mesh=mesh, in_specs=in_specs, out_specs=out_specs, check_vma=False,
    )
```

time: 517 us -> 200 us (0.39); the launches traced: 510 us -> 198 us
  other arithmetic: 226 us -> 0 us
  Pallas kernels: 0 us -> 196 us
  local copies, waits for them, and re-layouts: 149 us -> 2.14 us
  blocking collectives: 97.3 us -> 0 us
  waiting for transfers between devices: 17.8 us -> 0 us
  starting transfers between devices: 16.2 us -> 0 us
    pallas_call x0 -> x7, Pallas kernels: none -> 196 us  [the longest x1 59.5 us: body(): pl.pallas_call(second_kernel, out_shape=f32(BLK_DEV * ROWS, LANES), in_sp...]
    unnamed x1 -> x0, blocking collectives: 57.7 us -> none
    mul x13 -> x0, other arithmetic: 53.7 us -> none  [the longest x6 31.3 us: minmod(): 0.5 * (jnp.sign(first) + jnp.sign(second))]
    sub x18 -> x0, other arithmetic: 50.2 us -> none  [the longest x6 32.8 us: divergence(): right = trimmed(prims, along, 2, 1) - 0.5 * trimmed(slope, along, 1, 0)]
    reshape x4 -> x0, local copies, waits for them, and re-layouts: 45.5 us -> none  [the longest x1 15.2 us: body(): jnp.transpose(result, (1, 3, 5, 0, 2, 4, 6)).reshape(BLK_DEV, fields, cells)]
    pmax x1 -> x0, blocking collectives: 39.6 us -> none  [global_speed(): return lax.pmax(local_top, ('group', 'dev'))]
    div x13 -> x0, other arithmetic: 38.6 us -> none  [the longest x12 38.5 us: hlle_flux(): (upper * flux_left - lower * flux_right + upper * lower * (state_right -...]
    slice x14 -> x0, local copies, waits for them, and re-layouts: 34 us -> none  [the longest x6 15.6 us: trimmed(): lax.slice_in_dim(values, front, values.shape[along] - back, axis=along)]
  transfers between devices with their start and end apart: 9 -> 0, of which waited for: 4 -> 0; matrix products, arithmetic and copies ran while one was open for 4% -> 0% of each run, Pallas kernels for 0% -> 0%
where the time goes in v1:
time: 200 us; the launch traced here: 198 us
  Pallas kernels  196 us (98%)
  local copies, waits for them, and re-layouts  2.14 us (1%)
    pallas_call x1, Pallas kernels, body(): pl.pallas_call(second_kernel, out_shape=f32(BLK_DEV * ROWS, LANES), in_sp...  59.5 us
    pallas_call x1, Pallas kernels, body(): pl.pallas_call(first_kernel, out_shape=(f32(*SLAB), f32(*PACK), f32(*PACK...  56.7 us
    pallas_call x1, Pallas kernels, body(): pl.pallas_call(functools.partial(gather_kernel, groups, devs, cap), out_s...  43.8 us
    pallas_call x2, Pallas kernels, exchange(): pl.pallas_call(functools.partial(halo_kernel, groups, devs), out_shape=gh...  29.1 us

profile of v1, /device:TPU:1, one launch (start us, length us, event | category | flops | bytes accessed | tf_op | source)
XLA Modules:
  0.0 198.4 jit_solution(16577339269986938545)
XLA Ops:
  0.7 0.0 copy-start
  0.7 2.1 %copy-done = f32[31,8,4096]{2,1,0:T(8,128)S(1)} copy-done((f32[31,8,4096]{2,1,0:T(8,128)S(1)}, f32[31,8,4096]{2,1,0:T(8,128)}, u32[]{:S(2)}) %copy-start) | copy-done | bytes 4063256
  2.8 2.7 %stage.1.outgoing = f32[3840,128]{1,0:T(8,128)S(1)} custom-call(s32[1]{0:T(128)S(6)} %copy.3.count_ref, f32[7936,128]{1,0:T(8,128)S(1)} %bitcast.10), custom_call_target="tpu_custom_call" | custom-call | tf_op jit(solution)/shard_map/stage/pallas_call | solution.py:447
  5.5 43.8 %gather.1 = (f32[8,128]{1,0:T(8,128)S(1)}, s32[8,128]{1,0:T(8,128)S(1)}, f32[8192,128]{1,0:T(8,128)}) custom-call(s32[1]{0:T(128)S(6)} %copy.3.count_ref, f32[3840,128]{1,0:T(8,128)S(1)} %stage.1.outgoing, f32[7936,128]{1,0:T(8,128)S(1)} %bitcast.11), custom_call_target="tpu_custom_call" | custom-call | tf_op jit(solution)/shard_map/gather/pallas_call | solution.py:456
  49.3 3.8 %assemble.1 = (f32[16,8,4,8,128]{4,3,2,1,0:T(8,128)S(1)}, f32[16,2,8,128]{3,2,1,0:T(8,128)S(1)}, f32[16,2,8,128]{3,2,1,0:T(8,128)S(1)}) custom-call(s32[8,128]{1,0:T(8,128)S(1)} %get-tuple-element.23.small_ref, f32[8192,128]{1,0:T(8,128)} %get-tuple-element.24.joined), custom_call_target="tpu_custom_call" | custom-call | tf_op jit(solution)/shard_map/assemble/pallas_call | solution.py:481
  53.1 14.8 %halo.2 = (f32[2,8,4,8,128]{4,3,2,1,0:T(8,128)S(1)}, f32[2,8,4,8,128]{4,3,2,1,0:T(8,128)S(1)}, f32[16,2,8,128]{3,2,1,0:T(8,128)S(1)}, f32[16,2,8,128]{3,2,1,0:T(8,128)S(1)}) custom-call(f32[16,8,4,8,128]{4,3,2,1,0:T(8,128)S(1)} %get-tuple-element.25.u_ref, f32[16,2,8,128]{3,2,1,0:T(8,128)S(1)} %get-tuple-element.26.plo_ref, ...), custom_call_target="tpu_custom_call" | custom-call | tf_op jit(solution)/shard_map/halo/pallas_call | solution.py:491
  67.9 56.7 %first_stage.1 = (f32[16,8,4,8,128]{4,3,2,1,0:T(8,128)S(1)}, f32[16,2,8,128]{3,2,1,0:T(8,128)S(1)}, f32[16,2,8,128]{3,2,1,0:T(8,128)S(1)}) custom-call(f32[8,128]{1,0:T(8,128)S(1)} %get-tuple-element.22.step_ref, f32[16,8,4,8,128]{4,3,2,1,0:T(8,128)S(1)} %get-tuple-element.25.u_ref, f32[2,8,4,8,128]{4,3,2,1,0:T(8,128)S(1)} %get-tuple-element.28.xlo, ...), custom_call_target="tpu_custom_call" | custom-call | tf_op jit(solution)/shard_map/first_stage/pallas_call | solution.py:509
  124.6 14.3 %halo.3 = (f32[2,8,4,8,128]{4,3,2,1,0:T(8,128)S(1)}, f32[2,8,4,8,128]{4,3,2,1,0:T(8,128)S(1)}, f32[16,2,8,128]{3,2,1,0:T(8,128)S(1)}, f32[16,2,8,128]{3,2,1,0:T(8,128)S(1)}) custom-call(f32[16,8,4,8,128]{4,3,2,1,0:T(8,128)S(1)} %get-tuple-element.32.u_ref.one_ref, f32[16,2,8,128]{3,2,1,0:T(8,128)S(1)} %get-tuple-element.33.plo_ref, ...), custom_call_target="tpu_custom_call" | custom-call | tf_op jit(solution)/shard_map/halo/pallas_call | solution.py:491
  138.9 59.5 %second_stage.1 = f32[4096,128]{1,0:T(8,128)} custom-call(f32[8,128]{1,0:T(8,128)S(1)} %get-tuple-element.22.step_ref, f32[16,8,4,8,128]{4,3,2,1,0:T(8,128)S(1)} %get-tuple-element.25.u_ref, f32[16,8,4,8,128]{4,3,2,1,0:T(8,128)S(1)} %get-tuple-element.32.u_ref.one_ref, f32[2,8,4,8,128]{4,3,2,1,0:T(8,128)S(1)} %get-tuple-element.35.xlo, ...), custom_call_target="tpu_custom_call" | custom-call | tf_op jit(solution)/shard_map/second_stage/pallas_call | solution.py:520
Async XLA Ops:
  0.7 2.2 %copy-start = (f32[31,8,4096]{2,1,0:T(8,128)S(1)}, f32[31,8,4096]{2,1,0:T(8,128)}, u32[]{:S(2)}) copy-start(f32[31,8,4096]{2,1,0:T(8,128)} %param.2) | copy-start | bytes 12189700

commit v2 on v1

--- a/solution.py
+++ b/solution.py
@@ -26,9 +26,14 @@
 MESH = pl.DeviceIdType.MESH
 
 
+def reciprocal(x):
+    guess = pl.reciprocal(x, approx=True)
+    return guess * (2.0 - x * guess)
+
+
 def primitive(u):
     density = jnp.maximum(u[0], DENSITY_FLOOR)
-    inverse = 1.0 / density
+    inverse = reciprocal(density)
     vx, vy, vz = u[1] * inverse, u[2] * inverse, u[3] * inverse
     kinetic = 0.5 * density * (vx * vx + vy * vy + vz * vz)
     energy_b = 0.5 * (u[5] * u[5] + u[6] * u[6] + u[7] * u[7])
@@ -43,39 +48,40 @@
     return outer * lax.rsqrt(outer)
 
 
-def side(w, n):
+def wave(w, n):
+    inverse = reciprocal(w[0])
+    b2 = w[5] * w[5] + w[6] * w[6] + w[7] * w[7]
+    bn = w[5 + n]
+    return fast_from(GAMMA * w[4] * inverse, b2 * inverse, bn * bn * inverse), 0.5 * b2
+
+
+def weighted(w, half_b2, n, weight, shift):
     r, v, p, b = w[0], w[1:4], w[4], w[5:8]
-    inverse = 1.0 / r
-    b2 = b[0] * b[0] + b[1] * b[1] + b[2] * b[2]
-    v2 = v[0] * v[0] + v[1] * v[1] + v[2] * v[2]
-    half_b2 = 0.5 * b2
-    m = [r * v[0], r * v[1], r * v[2]]
-    energy = p * (1.0 / (GAMMA - 1.0)) + 0.5 * r * v2 + half_b2
-    total_p = p + half_b2
     vn, bn = v[n], b[n]
-    fast = fast_from(GAMMA * p * inverse, b2 * inverse, bn * bn * inverse)
+    k = weight * vn + shift
+    q = r * k
+    wb = weight * bn
+    wp = weight * (p + half_b2)
+    energy = p * (1.0 / (GAMMA - 1.0)) + half_b2 + 0.5 * r * (v[0] * v[0] + v[1] * v[1] + v[2] * v[2])
     vb = v[0] * b[0] + v[1] * b[1] + v[2] * b[2]
-    fm = [m[i] * vn - b[i] * bn for i in range(3)]
-    fm[n] = fm[n] + total_p
-    fe = (energy + total_p) * vn - bn * vb
-    fb = [None if i == n else vn * b[i] - v[i] * bn for i in range(3)]
-    return [r] + m + [energy] + b, [m[n]] + fm + [fe] + fb, vn, fast
+    momentum = [v[i] * q - b[i] * wb for i in range(3)]
+    momentum[n] = momentum[n] + wp
+    field = [shift * bn if i == n else b[i] * k - v[i] * wb for i in range(3)]
+    return [q] + momentum + [energy * k + wp * vn - wb * vb] + field
 
 
 def hlle(left, right, n):
-    ul, fl, vl, cl = side(left, n)
-    ur, fr, vr, cr = side(right, n)
+    cl, hl = wave(left, n)
+    cr, hr = wave(right, n)
+    vl, vr = left[1 + n], right[1 + n]
     upper = jnp.maximum(jnp.maximum(vr + cr, vl + cl), 0.0)
     lower = jnp.minimum(jnp.minimum(vl - cl, vr - cr), 0.0)
-    inverse = 1.0 / (upper - lower)
+    inverse = reciprocal(upper - lower)
     a = upper * inverse
-    b = lower * inverse
     c = a * lower
-    out = []
-    for f in range(FIELDS):
-        jump = c * (ur[f] - ul[f])
-        out.append(jump if fl[f] is None else a * fl[f] - b * fr[f] + jump)
-    return out
+    first = weighted(left, hl, n, a, -c)
+    second = weighted(right, hr, n, -lower * inverse, c)
+    return [x + y for x, y in zip(first, second)]
 
 
 def half_minmod(a, b):
@@ -92,21 +98,36 @@
     return lax.broadcasted_iota(jnp.int32, (8, LANES), 1)
 
 
-def z_up(x, last):
-    return jnp.where(last, roll(roll(x, 15, 1), -1, 0), roll(x, -1, 1))
-
-
-def z_down(x, first):
-    return jnp.where(first, roll(roll(x, -15, 1), 1, 0), roll(x, 1, 1))
+def lane_gather(x, index):
+    return jnp.take_along_axis(x, index, axis=1, mode="promise_in_bounds")
+
+
+def z_up(tiles):
+    lane = lane_index()
+    edge = lane % BS == 0
+    index = lane - lane % BS + (lane + 1) % BS
+    moved = [jnp.where(edge, roll(x, -1, 0), x) for x in tiles]
+    return jnp.stack([lane_gather(x, index) for x in moved])
+
+
+def z_down(tiles):
+    lane = lane_index()
+    edge = lane % BS == BS - 1
+    index = lane - lane % BS + (lane + BS - 1) % BS
+    moved = [jnp.where(edge, roll(x, 1, 0), x) for x in tiles]
+    return jnp.stack([lane_gather(x, index) for x in moved])
+
+
+def split(x):
+    return [x[i] for i in range(x.shape[0])]
 
 
 def fill_primitives(u_ref, xlo_ref, xhi_ref, glo_ref, ghi_ref, w_ref):
     def planes(source, base):
         def one(c, carry):
-            for v in range(YV):
-                w, _ = primitive([source[c, f, v] for f in range(FIELDS)])
-                for f in range(FIELDS):
-                    w_ref[base + c, f, v + 1] = w[f]
+            w, _ = primitive([source[c, f] for f in range(FIELDS)])
+            for f in range(FIELDS):
+                w_ref[base + c, f, 1:YV + 1] = w[f]
             return carry
 
         lax.fori_loop(0, source.shape[0], one, 0)
@@ -126,76 +147,82 @@
     lax.fori_loop(0, BS, ghosts, 0)
 
 
-def x_faces(w_ref, fx_ref):
-    for v in range(YV):
-        def one(face, slope):
-            left, right, after = [], [], []
-            for f in range(FIELDS):
-                here = w_ref[face + 1, f, v + 1]
-                there = w_ref[face + 2, f, v + 1]
-                beyond = w_ref[face + 3, f, v + 1]
-                new = half_minmod(there - here, beyond - there)
-                left.append(here + slope[f])
-                right.append(there - new)
-                after.append(new)
-            flux = hlle(left, right, 0)
-            for f in range(FIELDS):
-                fx_ref[face, f, v] = flux[f]
-            return tuple(after)
-
-        first = tuple(
-            half_minmod(
-                w_ref[1, f, v + 1] - w_ref[0, f, v + 1], w_ref[2, f, v + 1] - w_ref[1, f, v + 1]
+PAIRS = ((0, 2), (2, 2))
+
+
+def x_faces(w_ref, sx_ref, fx_ref):
+    def slopes(c, carry):
+        for f in range(FIELDS):
+            here = w_ref[c + 1, f, 1:YV + 1]
+            sx_ref[c, f] = half_minmod(
+                here - w_ref[c, f, 1:YV + 1], w_ref[c + 2, f, 1:YV + 1] - here
             )
-            for f in range(FIELDS)
-        )
-        lax.fori_loop(0, BS + 1, one, first)
-
-
-def y_faces(w_ref, c, f_ref):
-    lane = lane_index()
+        return carry
+
+    lax.fori_loop(0, BS + 2, slopes, 0)
+
+    def one(face, carry):
+        for v, n in PAIRS:
+            left = [w_ref[face + 1, f, v + 1:v + 1 + n] + sx_ref[face, f, v:v + n] for f in range(FIELDS)]
+            right = [
+                w_ref[face + 2, f, v + 1:v + 1 + n] - sx_ref[face + 1, f, v:v + n]
+                for f in range(FIELDS)
+            ]
+            for f, flux in enumerate(hlle(left, right, 0)):
+                fx_ref[face, f, v:v + n] = flux
+        return carry
+
+    lax.fori_loop(0, BS + 1, one, 0)
+
+
+def faces(l_ref, r_ref, f_ref, n, parts):
+    for v, size in parts:
+        left = [l_ref[f, v:v + size] for f in range(FIELDS)]
+        right = [r_ref[f, v:v + size] for f in range(FIELDS)]
+        for f, flux in enumerate(hlle(left, right, n)):
+            f_ref[f, v:v + size] = flux
+
+
+def y_faces(w_ref, c, l_ref, r_ref, f_ref):
+    lane = lax.broadcasted_iota(jnp.int32, (YV + 2, 8, LANES), 2)
     top = lane >= LANES - BS
     bottom = lane < BS
-    left = [[None] * FIELDS for _ in range(YV + 1)]
-    right = [[None] * FIELDS for _ in range(YV + 1)]
     for f in range(FIELDS):
-        w = [w_ref[c + 2, f, v] for v in range(YV + 2)]
-        rolled = [roll(x, -BS, 1) for x in w]
-        up = [jnp.where(top, rolled[min(v + 1, YV + 1)], rolled[v]) for v in range(YV + 2)]
-        diff = [up[v] - w[v] for v in range(YV + 2)]
-        rolled = [roll(x, BS, 1) for x in diff]
-        down = [jnp.where(bottom, rolled[max(v - 1, 0)], rolled[v]) for v in range(YV + 2)]
-        slope = [half_minmod(down[v], diff[v]) for v in range(YV + 2)]
-        low = [roll(w[v] - slope[v], -BS, 1) for v in range(YV + 2)]
-        for v in range(YV + 1):
-            left[v][f] = w[v] + slope[v]
-            right[v][f] = jnp.where(top, low[v + 1], low[v])
-    for v in range(YV + 1):
-        flux = hlle(left[v], right[v], 1)
-        for f in range(FIELDS):
-            f_ref[f, v] = flux[f]
-
-
-def tile_tendency(w_ref, fx_ref, fy_ref, c, v):
-    lane = lane_index()
-    bottom = lane < BS
-    cz = lane % BS
-    last, start = cz == BS - 1, cz == 0
-    left, right = [], []
+        w = w_ref[c + 2, f]
+        rolled = roll(w, -BS, 2)
+        diff = jnp.where(top, jnp.concatenate([rolled[1:], rolled[-1:]]), rolled) - w
+        rolled = roll(diff, BS, 2)
+        down = jnp.where(bottom, jnp.concatenate([rolled[:1], rolled[:-1]]), rolled)
+        slope = half_minmod(down, diff)
+        low = roll(w - slope, -BS, 2)
+        l_ref[f] = (w + slope)[:YV + 1]
+        r_ref[f] = jnp.where(top[1:], low[1:], low[:-1])
+    faces(l_ref, r_ref, f_ref, 1, PAIRS + ((YV, 1),))
+
+
+def z_faces(w_ref, c, l_ref, r_ref, f_ref):
     for f in range(FIELDS):
-        w = w_ref[c + 2, f, v + 1]
-        diff = z_up(w, last) - w
-        slope = half_minmod(z_down(diff, start), diff)
-        left.append(w + slope)
-        right.append(z_up(w - slope, last))
-    flux = hlle(left, right, 2)
+        w = w_ref[c + 2, f, 1:YV + 1]
+        diff = z_up(split(w)) - w
+        slope = half_minmod(z_down(split(diff)), diff)
+        l_ref[f, 0:YV] = w + slope
+        r_ref[f, 0:YV] = z_up(split(w - slope))
+    faces(l_ref, r_ref, f_ref, 2, PAIRS)
+
+
+def plane_change(w_ref, fx_ref, c, work):
+    ly, ry, fy, lz, rz, fz = work
+    y_faces(w_ref, c, ly, ry, fy)
+    z_faces(w_ref, c, lz, rz, fz)
+    bottom = lax.broadcasted_iota(jnp.int32, (YV, 8, LANES), 2) < BS
     out = []
     for f in range(FIELDS):
-        across_z = flux[f] - z_down(flux[f], start)
-        upper = fy_ref[f, v + 1]
-        across_y = upper - jnp.where(bottom, roll(fy_ref[f, v], BS, 1), roll(upper, BS, 1))
-        across_x = fx_ref[c + 1, f, v] - fx_ref[c, f, v]
-        out.append(across_x + across_y + across_z)
+        flux = fz[f]
+        across_z = flux - z_down(split(flux))
+        flux = fy[f]
+        rolled = roll(flux, BS, 2)
+        across_y = flux[1:] - jnp.where(bottom, rolled[:-1], rolled[1:])
+        out.append((fx_ref[c + 1, f] - fx_ref[c, f]) + across_y + across_z)
     return out
 
 
@@ -210,42 +237,44 @@
     return out
 
 
-def first_kernel(step_ref, u_ref, xlo, xhi, glo, ghi, out_ref, plo_ref, phi_ref, w_ref, fx_ref, fy_ref):
+def first_kernel(
+    step_ref, u_ref, xlo, xhi, glo, ghi, out_ref, plo_ref, phi_ref, w_ref, sx_ref, fx_ref, *work
+):
     fill_primitives(u_ref, xlo, xhi, glo, ghi, w_ref)
-    x_faces(w_ref, fx_ref)
+    x_faces(w_ref, sx_ref, fx_ref)
 
     def one(c, carry):
         step = step_ref[...]
-        y_faces(w_ref, c, fy_ref)
-        for v in range(YV):
-            change = tile_tendency(w_ref, fx_ref, fy_ref, c, v)
-            new = [u_ref[c, f, v] - step * change[f] for f in range(FIELDS)]
-            for f in range(FIELDS):
-                out_ref[c, f, v] = new[f]
-            if v == 0:
-                for q, tile in enumerate(pack(new, 0)):
-                    plo_ref[c, q] = tile
-            if v == YV - 1:
-                for q, tile in enumerate(pack(new, 96)):
-                    phi_ref[c, q] = tile
+        change = plane_change(w_ref, fx_ref, c, work)
+        low, high = [], []
+        for f in range(FIELDS):
+            new = u_ref[c, f] - step * change[f]
+            out_ref[c, f] = new
+            low.append(new[0])
+            high.append(new[YV - 1])
+        for q, tile in enumerate(pack(low, 0)):
+            plo_ref[c, q] = tile
+        for q, tile in enumerate(pack(high, 96)):
+            phi_ref[c, q] = tile
         return carry
 
     lax.fori_loop(0, BS, one, 0)
 
 
-def second_kernel(step_ref, u_ref, one_ref, xlo, xhi, glo, ghi, out_ref, w_ref, fx_ref, fy_ref):
+def second_kernel(
+    step_ref, u_ref, one_ref, xlo, xhi, glo, ghi, out_ref, w_ref, sx_ref, fx_ref, *work
+):
     fill_primitives(one_ref, xlo, xhi, glo, ghi, w_ref)
-    x_faces(w_ref, fx_ref)
+    x_faces(w_ref, sx_ref, fx_ref)
 
     def one(c, carry):
         step = step_ref[...]
-        y_faces(w_ref, c, fy_ref)
-        for v in range(YV):
-            change = tile_tendency(w_ref, fx_ref, fy_ref, c, v)
-            for f in range(FIELDS):
-                new = 0.5 * (u_ref[c, f, v] + one_ref[c, f, v] - step * change[f])
+        change = plane_change(w_ref, fx_ref, c, work)
+        for f in range(FIELDS):
+            new = 0.5 * (u_ref[c, f] + one_ref[c, f] - step * change[f])
+            for v in range(YV):
                 row = (v // 2) * (BRICK_Z * ROWS) + (c * 2 + v % 2) * FIELDS + f
-                out_ref[pl.ds(row, BRICK_Z, stride=ROWS), :] = new
+                out_ref[pl.ds(row, BRICK_Z, stride=ROWS), :] = new[v]
         return carry
 
     lax.fori_loop(0, BS, one, 0)
@@ -277,8 +306,12 @@
     )
 
 
-def spread(source, slots, send, recv, peers):
-    copies = [remote(source, slots.at[d], send.at[d], recv.at[d], p) for d, p in enumerate(peers)]
+def spread(*messages):
+    copies = [
+        remote(source, slots.at[d], send.at[d], recv.at[d], p)
+        for source, slots, send, recv, peers in messages
+        for d, p in enumerate(peers)
+    ]
     for copy in copies:
         copy.start()
     for copy in copies:
@@ -341,10 +374,12 @@
     groups, devs, cap, count_ref, outgoing, own_ref,
     step_ref, small_ref, joined,
     count_msg, count_row, count_col, speed_msg, speed_row, speed_col,
-    total_ref, block_sem, row_send, row_recv, col_send, col_recv,
+    total_ref, held, block_sem, row_send, row_recv, col_send, col_recv,
     srow_send, srow_recv, scol_send, scol_recv, local_sem,
 ):
     g, j, me, curve_next, curve_prev, row, column = ring(groups, devs)
+    staged = pltpu.make_async_copy(own_ref, held, local_sem.at[2])
+    staged.start()
     greet(row + column + [curve_next, curve_prev])
     count = count_ref[0]
     blocks = remote(
@@ -357,43 +392,46 @@
         local_sem.at[0],
     )
     local.start()
+    staged.wait()
+
+    slot = lax.broadcasted_iota(jnp.int32, (8, LANES), 0)
+
+    def chunk(t, top):
+        for first in list(range(0, cap - 8, 8)) + [cap - 8]:
+            u = [
+                held[pl.ds(first * ROWS + t * FIELDS + f, 8, stride=ROWS), :]
+                for f in range(FIELDS)
+            ]
+            top = jnp.maximum(top, jnp.where(slot + first < count, signal_speed(u), 0.0))
+        return top
+
+    top = lax.fori_loop(0, CHUNKS, chunk, jnp.zeros((8, LANES), jnp.float32))
 
     count_msg[...] = jnp.full((8, LANES), count, jnp.int32)
-    spread(count_msg, count_row, row_send, row_recv, row)
+    speed_msg[...] = top
+    spread(
+        (count_msg, count_row, row_send, row_recv, row),
+        (speed_msg, speed_row, srow_send, srow_recv, row),
+    )
     before = jnp.zeros((8, LANES), jnp.int32)
     every = count_msg[...]
     for d in range(1, devs):
         value = count_row[d - 1]
         every = every + value
         before = before + jnp.where(d <= j, value, 0)
+        top = jnp.maximum(top, speed_row[d - 1])
     count_msg[...] = every
-    spread(count_msg, count_col, col_send, col_recv, column)
+    speed_msg[...] = top
+    spread(
+        (count_msg, count_col, col_send, col_recv, column),
+        (speed_msg, speed_col, scol_send, scol_recv, column),
+    )
     for d in range(1, groups):
         before = before + jnp.where(d <= g, count_col[d - 1], 0)
+        top = jnp.maximum(top, speed_col[d - 1])
     total_ref[...] = before - me * BLK_DEV
     narrow = pltpu.make_async_copy(total_ref, small_ref, local_sem.at[1])
     narrow.start()
-
-    slot = lax.broadcasted_iota(jnp.int32, (8, LANES), 0)
-
-    def chunk(t, top):
-        for first in list(range(0, cap - 8, 8)) + [cap - 8]:
-            u = [
-                own_ref[pl.ds(first * ROWS + t * FIELDS + f, 8, stride=ROWS), :]
-                for f in range(FIELDS)
-            ]
-            top = jnp.maximum(top, jnp.where(slot + first < count, signal_speed(u), 0.0))
-        return top
-
-    top = lax.fori_loop(0, CHUNKS, chunk, jnp.zeros((8, LANES), jnp.float32))
-    speed_msg[...] = top
-    spread(speed_msg, speed_row, srow_send, srow_recv, row)
-    for d in range(devs - 1):
-        top = jnp.maximum(top, speed_row[d])
-    speed_msg[...] = top
-    spread(speed_msg, speed_col, scol_send, scol_recv, column)
-    for d in range(groups - 1):
-        top = jnp.maximum(top, speed_col[d])
     top = jnp.max(jnp.max(top, axis=1, keepdims=True), axis=0, keepdims=True)
     step_ref[...] = COURANT / jnp.broadcast_to(top, (8, LANES))
 
@@ -458,7 +496,7 @@
         out_shape=(
             f32(*TILE), jax.ShapeDtypeStruct(TILE, jnp.int32), f32(2 * BLK_DEV * ROWS, LANES)
         ),
-        in_specs=[SMEM, VMEM, VMEM],
+        in_specs=[SMEM, VMEM, ANY],
         out_specs=(VMEM, SMEM, VMEM),
         scratch_shapes=[
             pltpu.VMEM(TILE, jnp.int32),
@@ -468,10 +506,11 @@
             pltpu.VMEM((devs - 1,) + TILE, jnp.float32),
             pltpu.VMEM((groups - 1,) + TILE, jnp.float32),
             pltpu.VMEM(TILE, jnp.int32),
+            pltpu.VMEM((cap * ROWS, LANES), jnp.float32),
             dma((2,)),
             dma((devs - 1,)), dma((devs - 1,)), dma((groups - 1,)), dma((groups - 1,)),
             dma((devs - 1,)), dma((devs - 1,)), dma((groups - 1,)), dma((groups - 1,)),
-            dma((2,)),
+            dma((3,)),
         ],
         compiler_params=pltpu.CompilerParams(
             collective_id=0, has_side_effects=True, vmem_limit_bytes=LIMIT
@@ -503,9 +542,11 @@
     xlo, xhi, glo, ghi = exchange(u, plo, phi, 1)
     work = [
         pltpu.VMEM((BS + 4, FIELDS, YV + 2) + TILE, jnp.float32),
+        pltpu.VMEM((BS + 2, FIELDS, YV) + TILE, jnp.float32),
         pltpu.VMEM((BS + 1, FIELDS, YV) + TILE, jnp.float32),
-        pltpu.VMEM((FIELDS, YV + 1) + TILE, jnp.float32),
-    ]
+    ] + [pltpu.VMEM((FIELDS, YV + 1) + TILE, jnp.float32)] * 3 + [
+        pltpu.VMEM((FIELDS, YV) + TILE, jnp.float32)
+    ] * 3
     one, plo, phi = pl.pallas_call(
         first_kernel,
         out_shape=(f32(*SLAB), f32(*PACK), f32(*PACK)),

time: 200 us -> 142 us (0.71)
  Pallas kernels: 196 us -> 138 us
    pallas_call x1, Pallas kernels: 59.5 us -> 34.6 us  [body(): pl.pallas_call(second_kernel, out_shape=f32(BLK_DEV * ROWS, LANES), in_sp...]
    pallas_call x1, Pallas kernels: 56.7 us -> 32 us  [body(): pl.pallas_call(first_kernel, out_shape=(f32(*SLAB), f32(*PACK), f32(*PACK...]
    pallas_call x1, Pallas kernels: 43.8 us -> 35.7 us  [body(): pl.pallas_call(functools.partial(gather_kernel, groups, devs, cap), out_s...]
where the time goes in v2:
time: 142 us; the launch traced here: 141 us
  Pallas kernels  138 us (97%)
  local copies, waits for them, and re-layouts  2.14 us (2%)
    pallas_call x1, Pallas kernels, body(): pl.pallas_call(functools.partial(gather_kernel, groups, devs, cap), out_s...  35.7 us
    pallas_call x1, Pallas kernels, body(): pl.pallas_call(second_kernel, out_shape=f32(BLK_DEV * ROWS, LANES), in_sp...  34.6 us
    pallas_call x1, Pallas kernels, body(): pl.pallas_call(first_kernel, out_shape=(f32(*SLAB), f32(*PACK), f32(*PACK...  32 us
    pallas_call x2, Pallas kernels, exchange(): pl.pallas_call(functools.partial(halo_kernel, groups, devs), out_shape=gh...  29.1 us
    pallas_call x1, Pallas kernels, body(): pl.pallas_call(assemble_kernel, out_shape=(f32(*SLAB), f32(*PACK), f32(*P...  3.81 us

profile of v2, /device:TPU:1, one launch (start us, length us, event | category | flops | bytes accessed | tf_op | source)
XLA Modules:
  0.0 140.6 jit_solution(14389918299442153047)
XLA Ops:
  0.7 0.0 copy-start
  0.7 2.1 %copy-done = f32[31,8,4096]{2,1,0:T(8,128)S(1)} copy-done((f32[31,8,4096]{2,1,0:T(8,128)S(1)}, f32[31,8,4096]{2,1,0:T(8,128)}, u32[]{:S(2)}) %copy-start) | copy-done | bytes 4063256
  2.8 2.7 %stage.1.outgoing = f32[3840,128]{1,0:T(8,128)S(1)} custom-call(s32[1]{0:T(128)S(6)} %copy.3.count_ref, f32[7936,128]{1,0:T(8,128)S(1)} %bitcast.10), custom_call_target="tpu_custom_call" | custom-call | tf_op jit(solution)/shard_map/stage/pallas_call | solution.py:485
  5.5 35.7 %gather.1 = (f32[8,128]{1,0:T(8,128)S(1)}, s32[8,128]{1,0:T(8,128)S(1)}, f32[8192,128]{1,0:T(8,128)}) custom-call(s32[1]{0:T(128)S(6)} %copy.3.count_ref, f32[3840,128]{1,0:T(8,128)S(1)} %stage.1.outgoing, f32[7936,128]{1,0:T(8,128)S(1)} %bitcast.11), custom_call_target="tpu_custom_call" | custom-call | tf_op jit(solution)/shard_map/gather/pallas_call | solution.py:494
  41.2 3.8 %assemble.1 = (f32[16,8,4,8,128]{4,3,2,1,0:T(8,128)S(1)}, f32[16,2,8,128]{3,2,1,0:T(8,128)S(1)}, f32[16,2,8,128]{3,2,1,0:T(8,128)S(1)}) custom-call(s32[8,128]{1,0:T(8,128)S(1)} %get-tuple-element.23.small_ref, f32[8192,128]{1,0:T(8,128)} %get-tuple-element.24.joined), custom_call_target="tpu_custom_call" | custom-call | tf_op jit(solution)/shard_map/assemble/pallas_call | solution.py:520
  45.0 12.9 %halo.2 = (f32[2,8,4,8,128]{4,3,2,1,0:T(8,128)S(1)}, f32[2,8,4,8,128]{4,3,2,1,0:T(8,128)S(1)}, f32[16,2,8,128]{3,2,1,0:T(8,128)S(1)}, f32[16,2,8,128]{3,2,1,0:T(8,128)S(1)}) custom-call(f32[16,8,4,8,128]{4,3,2,1,0:T(8,128)S(1)} %get-tuple-element.25.u_ref, f32[16,2,8,128]{3,2,1,0:T(8,128)S(1)} %get-tuple-element.26.plo_ref, ...), custom_call_target="tpu_custom_call" | custom-call | tf_op jit(solution)/shard_map/halo/pallas_call | solution.py:530
  57.9 32.0 %first_stage.1 = (f32[16,8,4,8,128]{4,3,2,1,0:T(8,128)S(1)}, f32[16,2,8,128]{3,2,1,0:T(8,128)S(1)}, f32[16,2,8,128]{3,2,1,0:T(8,128)S(1)}) custom-call(f32[8,128]{1,0:T(8,128)S(1)} %get-tuple-element.22.step_ref, f32[16,8,4,8,128]{4,3,2,1,0:T(8,128)S(1)} %get-tuple-element.25.u_ref, f32[2,8,4,8,128]{4,3,2,1,0:T(8,128)S(1)} %get-tuple-element.28.xlo, ...), custom_call_target="tpu_custom_call" | custom-call | tf_op jit(solution)/shard_map/first_stage/pallas_call | solution.py:550
  89.9 16.2 %halo.3 = (f32[2,8,4,8,128]{4,3,2,1,0:T(8,128)S(1)}, f32[2,8,4,8,128]{4,3,2,1,0:T(8,128)S(1)}, f32[16,2,8,128]{3,2,1,0:T(8,128)S(1)}, f32[16,2,8,128]{3,2,1,0:T(8,128)S(1)}) custom-call(f32[16,8,4,8,128]{4,3,2,1,0:T(8,128)S(1)} %get-tuple-element.32.u_ref.one_ref, f32[16,2,8,128]{3,2,1,0:T(8,128)S(1)} %get-tuple-element.33.plo_ref, ...), custom_call_target="tpu_custom_call" | custom-call | tf_op jit(solution)/shard_map/halo/pallas_call | solution.py:530
  106.0 34.6 %second_stage.1 = f32[4096,128]{1,0:T(8,128)} custom-call(f32[8,128]{1,0:T(8,128)S(1)} %get-tuple-element.22.step_ref, f32[16,8,4,8,128]{4,3,2,1,0:T(8,128)S(1)} %get-tuple-element.25.u_ref, f32[16,8,4,8,128]{4,3,2,1,0:T(8,128)S(1)} %get-tuple-element.32.u_ref.one_ref, f32[2,8,4,8,128]{4,3,2,1,0:T(8,128)S(1)} %get-tuple-element.35.xlo, ...), custom_call_target="tpu_custom_call" | custom-call | tf_op jit(solution)/shard_map/second_stage/pallas_call | solution.py:561
Async XLA Ops:
  0.7 2.2 %copy-start = (f32[31,8,4096]{2,1,0:T(8,128)S(1)}, f32[31,8,4096]{2,1,0:T(8,128)}, u32[]{:S(2)}) copy-start(f32[31,8,4096]{2,1,0:T(8,128)} %param.2) | copy-start | bytes 12189700

commit v3 on v2

--- a/solution.py
+++ b/solution.py
@@ -122,21 +122,18 @@
     return [x[i] for i in range(x.shape[0])]
 
 
-def fill_primitives(u_ref, xlo_ref, xhi_ref, glo_ref, ghi_ref, w_ref):
-    def planes(source, base):
-        def one(c, carry):
-            w, _ = primitive([source[c, f] for f in range(FIELDS)])
-            for f in range(FIELDS):
-                w_ref[base + c, f, 1:YV + 1] = w[f]
-            return carry
-
-        lax.fori_loop(0, source.shape[0], one, 0)
-
-    planes(xlo_ref, 0)
-    planes(u_ref, 2)
-    planes(xhi_ref, 2 + BS)
-
-    def ghosts(c, carry):
+def fill_planes(source, w_ref, base):
+    def one(c, carry):
+        w, _ = primitive([source[c, f] for f in range(FIELDS)])
+        for f in range(FIELDS):
+            w_ref[base + c, f, 1:YV + 1] = w[f]
+        return carry
+
+    lax.fori_loop(0, source.shape[0], one, 0)
+
+
+def fill_ghosts(glo_ref, ghi_ref, w_ref):
+    def one(c, carry):
         for ghost, v, base in ((glo_ref, 0, 96), (ghi_ref, YV + 1, 0)):
             u = [roll(ghost[c, f // 4], base - 32 * (f % 4), 1) for f in range(FIELDS)]
             w, _ = primitive(u)
@@ -144,7 +141,7 @@
                 w_ref[c + 2, f, v] = w[f]
         return carry
 
-    lax.fori_loop(0, BS, ghosts, 0)
+    lax.fori_loop(0, BS, one, 0)
 
 
 PAIRS = ((0, 2), (2, 2))
@@ -210,20 +207,30 @@
     faces(l_ref, r_ref, f_ref, 2, PAIRS)
 
 
-def plane_change(w_ref, fx_ref, c, work):
-    ly, ry, fy, lz, rz, fz = work
-    y_faces(w_ref, c, ly, ry, fy)
-    z_faces(w_ref, c, lz, rz, fz)
+def z_pass(w_ref, acc_ref, lz, rz, fz):
+    def one(c, carry):
+        z_faces(w_ref, c, lz, rz, fz)
+        for f in range(FIELDS):
+            flux = fz[f]
+            acc_ref[c, f] = flux - z_down(split(flux))
+        return carry
+
+    lax.fori_loop(0, BS, one, 0)
+
+
+def y_pass(w_ref, acc_ref, ly, ry, fy):
     bottom = lax.broadcasted_iota(jnp.int32, (YV, 8, LANES), 2) < BS
-    out = []
-    for f in range(FIELDS):
-        flux = fz[f]
-        across_z = flux - z_down(split(flux))
-        flux = fy[f]
-        rolled = roll(flux, BS, 2)
-        across_y = flux[1:] - jnp.where(bottom, rolled[:-1], rolled[1:])
-        out.append((fx_ref[c + 1, f] - fx_ref[c, f]) + across_y + across_z)
-    return out
+
+    def one(c, carry):
+        y_faces(w_ref, c, ly, ry, fy)
+        for f in range(FIELDS):
+            flux = fy[f]
+            rolled = roll(flux, BS, 2)
+            across = flux[1:] - jnp.where(bottom, rolled[:-1], rolled[1:])
+            acc_ref[c, f] = across + acc_ref[c, f]
+        return carry
+
+    lax.fori_loop(0, BS, one, 0)
 
 
 def pack(tiles, base):
@@ -235,49 +242,6 @@
             total = jnp.where(group == k, roll(tiles[4 * q + k], 32 * k - base, 1), total)
         out.append(total)
     return out
-
-
-def first_kernel(
-    step_ref, u_ref, xlo, xhi, glo, ghi, out_ref, plo_ref, phi_ref, w_ref, sx_ref, fx_ref, *work
-):
-    fill_primitives(u_ref, xlo, xhi, glo, ghi, w_ref)
-    x_faces(w_ref, sx_ref, fx_ref)
-
-    def one(c, carry):
-        step = step_ref[...]
-        change = plane_change(w_ref, fx_ref, c, work)
-        low, high = [], []
-        for f in range(FIELDS):
-            new = u_ref[c, f] - step * change[f]
-            out_ref[c, f] = new
-            low.append(new[0])
-            high.append(new[YV - 1])
-        for q, tile in enumerate(pack(low, 0)):
-            plo_ref[c, q] = tile
-        for q, tile in enumerate(pack(high, 96)):
-            phi_ref[c, q] = tile
-        return carry
-
-    lax.fori_loop(0, BS, one, 0)
-
-
-def second_kernel(
-    step_ref, u_ref, one_ref, xlo, xhi, glo, ghi, out_ref, w_ref, sx_ref, fx_ref, *work
-):
-    fill_primitives(one_ref, xlo, xhi, glo, ghi, w_ref)
-    x_faces(w_ref, sx_ref, fx_ref)
-
-    def one(c, carry):
-        step = step_ref[...]
-        change = plane_change(w_ref, fx_ref, c, work)
-        for f in range(FIELDS):
-            new = 0.5 * (u_ref[c, f] + one_ref[c, f] - step * change[f])
-            for v in range(YV):
-                row = (v // 2) * (BRICK_Z * ROWS) + (c * 2 + v % 2) * FIELDS + f
-                out_ref[pl.ds(row, BRICK_Z, stride=ROWS), :] = new[v]
-        return carry
-
-    lax.fori_loop(0, BS, one, 0)
 
 
 def ring(groups, devs):
@@ -306,44 +270,128 @@
     )
 
 
-def spread(*messages):
-    copies = [
-        remote(source, slots.at[d], send.at[d], recv.at[d], p)
-        for source, slots, send, recv, peers in messages
-        for d, p in enumerate(peers)
-    ]
+def messages(source, slots, send, recv, peers):
+    return [remote(source, slots.at[d], send.at[d], recv.at[d], p) for d, p in enumerate(peers)]
+
+
+def begin(copies):
     for copy in copies:
         copy.start()
+
+
+def finish(copies):
     for copy in copies:
         copy.wait()
 
 
-def halo(g, j, groups, devs, u_ref, plo_ref, phi_ref, xlo, xhi, glo, ghi, send, recv):
+def step_kernel(
+    groups, devs, top_ref, u_ref, plo, phi, out_ref,
+    w_ref, sx_ref, fx_ref, acc_ref, one_ref, edge_lo, edge_hi, plo2, phi2,
+    xlo, xhi, glo, ghi, xlo2, xhi2, glo2, ghi2, ly, ry, fy, lz, rz, fz,
+    speed_msg, speed_row, speed_col, step_ref,
+    row_send, row_recv, col_send, col_recv, send, recv, send2, recv2,
+):
+    g, j, _, _, _, row, column = ring(groups, devs)
+    greet(row + column)
     up = (lax.rem(g + 1, groups), j)
     down = (lax.rem(g + groups - 1, groups), j)
     right = (g, lax.rem(j + 1, devs))
     left = (g, lax.rem(j + devs - 1, devs))
-    copies = [
+    speeds = messages(top_ref, speed_row, row_send, row_recv, row)
+    begin(speeds)
+    y_copies = [
+        remote(phi, glo, send.at[2], recv.at[2], right),
+        remote(plo, ghi, send.at[3], recv.at[3], left),
+    ]
+    begin(y_copies)
+    x_copies = [
         remote(u_ref.at[pl.ds(BS - 2, 2)], xlo, send.at[0], recv.at[0], up),
         remote(u_ref.at[pl.ds(0, 2)], xhi, send.at[1], recv.at[1], down),
-        remote(phi_ref, glo, send.at[2], recv.at[2], right),
-        remote(plo_ref, ghi, send.at[3], recv.at[3], left),
     ]
-    for copy in copies:
-        copy.start()
-    for copy in copies:
-        copy.wait()
-
-
-def halo_kernel(groups, devs, u_ref, plo_ref, phi_ref, xlo, xhi, glo, ghi, send, recv):
-    g, j = lax.axis_index("group"), lax.axis_index("dev")
-    greet([
-        (lax.rem(g + 1, groups), j),
-        (lax.rem(g + groups - 1, groups), j),
-        (g, lax.rem(j + 1, devs)),
-        (g, lax.rem(j + devs - 1, devs)),
-    ])
-    halo(g, j, groups, devs, u_ref, plo_ref, phi_ref, xlo, xhi, glo, ghi, send, recv)
+    begin(x_copies)
+
+    fill_planes(u_ref, w_ref, 2)
+    z_pass(w_ref, acc_ref, lz, rz, fz)
+
+    finish(speeds)
+    top = top_ref[...]
+    for d in range(devs - 1):
+        top = jnp.maximum(top, speed_row[d])
+    speed_msg[...] = top
+    speeds = messages(speed_msg, speed_col, col_send, col_recv, column)
+    begin(speeds)
+
+    finish(y_copies)
+    fill_ghosts(glo, ghi, w_ref)
+    y_pass(w_ref, acc_ref, ly, ry, fy)
+    finish(x_copies)
+    fill_planes(xlo, w_ref, 0)
+    fill_planes(xhi, w_ref, BS + 2)
+    x_faces(w_ref, sx_ref, fx_ref)
+
+    finish(speeds)
+    top = speed_msg[...]
+    for d in range(groups - 1):
+        top = jnp.maximum(top, speed_col[d])
+    top = jnp.max(jnp.max(top, axis=1, keepdims=True), axis=0, keepdims=True)
+    step_ref[...] = COURANT / jnp.broadcast_to(top, (8, LANES))
+
+    def update(c, edge, place):
+        step = step_ref[...]
+        low, high = [], []
+        for f in range(FIELDS):
+            change = (fx_ref[c + 1, f] - fx_ref[c, f]) + acc_ref[c, f]
+            new = u_ref[c, f] - step * change
+            one_ref[c, f] = new
+            if edge is not None:
+                edge[place, f] = new
+            low.append(new[0])
+            high.append(new[YV - 1])
+        for q, tile in enumerate(pack(low, 0)):
+            plo2[c, q] = tile
+        for q, tile in enumerate(pack(high, 96)):
+            phi2[c, q] = tile
+
+    def middle(c, carry):
+        update(c, None, 0)
+        return carry
+
+    for place in range(2):
+        update(place, edge_lo, place)
+        update(BS - 2 + place, edge_hi, place)
+    x_copies = [
+        remote(edge_hi, xlo2, send2.at[0], recv2.at[0], up),
+        remote(edge_lo, xhi2, send2.at[1], recv2.at[1], down),
+    ]
+    begin(x_copies)
+    lax.fori_loop(2, BS - 2, middle, 0)
+    y_copies = [
+        remote(phi2, glo2, send2.at[2], recv2.at[2], right),
+        remote(plo2, ghi2, send2.at[3], recv2.at[3], left),
+    ]
+    begin(y_copies)
+
+    fill_planes(one_ref, w_ref, 2)
+    z_pass(w_ref, acc_ref, lz, rz, fz)
+    finish(y_copies)
+    fill_ghosts(glo2, ghi2, w_ref)
+    y_pass(w_ref, acc_ref, ly, ry, fy)
+    finish(x_copies)
+    fill_planes(xlo2, w_ref, 0)
+    fill_planes(xhi2, w_ref, BS + 2)
+    x_faces(w_ref, sx_ref, fx_ref)
+
+    def last(c, carry):
+        step = step_ref[...]
+        for f in range(FIELDS):
+            change = (fx_ref[c + 1, f] - fx_ref[c, f]) + acc_ref[c, f]
+            new = 0.5 * (u_ref[c, f] + one_ref[c, f] - step * change)
+            for v in range(YV):
+                row = (v // 2) * (BRICK_Z * ROWS) + (c * 2 + v % 2) * FIELDS + f
+                out_ref[pl.ds(row, BRICK_Z, stride=ROWS), :] = new[v]
+        return carry
+
+    lax.fori_loop(0, BS, last, 0)
 
 
 def signal_speed(u):
@@ -372,16 +420,18 @@
 
 def gather_kernel(
     groups, devs, cap, count_ref, outgoing, own_ref,
-    step_ref, small_ref, joined,
-    count_msg, count_row, count_col, speed_msg, speed_row, speed_col,
-    total_ref, held, block_sem, row_send, row_recv, col_send, col_recv,
-    srow_send, srow_recv, scol_send, scol_recv, local_sem,
+    top_ref, small_ref, joined,
+    count_msg, row_msg, count_row, count_col, total_ref, held,
+    block_sem, row_send, row_recv, col_send, col_recv, local_sem,
 ):
     g, j, me, curve_next, curve_prev, row, column = ring(groups, devs)
     staged = pltpu.make_async_copy(own_ref, held, local_sem.at[2])
     staged.start()
     greet(row + column + [curve_next, curve_prev])
     count = count_ref[0]
+    count_msg[...] = jnp.full((8, LANES), count, jnp.int32)
+    counts = messages(count_msg, count_row, row_send, row_recv, row)
+    begin(counts)
     blocks = remote(
         outgoing, joined.at[pl.ds(ROWS, (BLK_DEV - 1) * ROWS)], block_sem.at[0], block_sem.at[1],
         curve_next,
@@ -392,8 +442,19 @@
         local_sem.at[0],
     )
     local.start()
+
+    finish(counts)
+    before = jnp.zeros((8, LANES), jnp.int32)
+    every = count_msg[...]
+    for d in range(1, devs):
+        value = count_row[d - 1]
+        every = every + value
+        before = before + jnp.where(d <= j, value, 0)
+    row_msg[...] = every
+    counts = messages(row_msg, count_col, col_send, col_recv, column)
+    begin(counts)
+
     staged.wait()
-
     slot = lax.broadcasted_iota(jnp.int32, (8, LANES), 0)
 
     def chunk(t, top):
@@ -405,36 +466,14 @@
             top = jnp.maximum(top, jnp.where(slot + first < count, signal_speed(u), 0.0))
         return top
 
-    top = lax.fori_loop(0, CHUNKS, chunk, jnp.zeros((8, LANES), jnp.float32))
-
-    count_msg[...] = jnp.full((8, LANES), count, jnp.int32)
-    speed_msg[...] = top
-    spread(
-        (count_msg, count_row, row_send, row_recv, row),
-        (speed_msg, speed_row, srow_send, srow_recv, row),
-    )
-    before = jnp.zeros((8, LANES), jnp.int32)
-    every = count_msg[...]
-    for d in range(1, devs):
-        value = count_row[d - 1]
-        every = every + value
-        before = before + jnp.where(d <= j, value, 0)
-        top = jnp.maximum(top, speed_row[d - 1])
-    count_msg[...] = every
-    speed_msg[...] = top
-    spread(
-        (count_msg, count_col, col_send, col_recv, column),
-        (speed_msg, speed_col, scol_send, scol_recv, column),
-    )
+    top_ref[...] = lax.fori_loop(0, CHUNKS, chunk, jnp.zeros((8, LANES), jnp.float32))
+
+    finish(counts)
     for d in range(1, groups):
         before = before + jnp.where(d <= g, count_col[d - 1], 0)
-        top = jnp.maximum(top, speed_col[d - 1])
     total_ref[...] = before - me * BLK_DEV
     narrow = pltpu.make_async_copy(total_ref, small_ref, local_sem.at[1])
     narrow.start()
-    top = jnp.max(jnp.max(top, axis=1, keepdims=True), axis=0, keepdims=True)
-    step_ref[...] = COURANT / jnp.broadcast_to(top, (8, LANES))
-
     narrow.wait()
     local.wait()
     blocks.wait()
@@ -479,7 +518,6 @@
     cap = blocks_in.shape[0]
     rows = blocks_in.reshape(cap, FIELDS, CHUNKS, LANES).transpose(0, 2, 1, 3)
     rows = rows.reshape(cap * ROWS, LANES)
-    ghosts = (f32(*EDGE), f32(*EDGE), f32(*PACK), f32(*PACK))
     dma = pltpu.SemaphoreType.DMA
     plain = pltpu.CompilerParams(vmem_limit_bytes=LIMIT)
     outgoing = pl.pallas_call(
@@ -491,7 +529,7 @@
         compiler_params=plain,
         name="stage",
     )(counts, rows)
-    step, small, joined = pl.pallas_call(
+    top, small, joined = pl.pallas_call(
         functools.partial(gather_kernel, groups, devs, cap),
         out_shape=(
             f32(*TILE), jax.ShapeDtypeStruct(TILE, jnp.int32), f32(2 * BLK_DEV * ROWS, LANES)
@@ -500,15 +538,12 @@
         out_specs=(VMEM, SMEM, VMEM),
         scratch_shapes=[
             pltpu.VMEM(TILE, jnp.int32),
+            pltpu.VMEM(TILE, jnp.int32),
             pltpu.VMEM((devs - 1,) + TILE, jnp.int32),
             pltpu.VMEM((groups - 1,) + TILE, jnp.int32),
-            pltpu.VMEM(TILE, jnp.float32),
-            pltpu.VMEM((devs - 1,) + TILE, jnp.float32),
-            pltpu.VMEM((groups - 1,) + TILE, jnp.float32),
             pltpu.VMEM(TILE, jnp.int32),
             pltpu.VMEM((cap * ROWS, LANES), jnp.float32),
             dma((2,)),
-            dma((devs - 1,)), dma((devs - 1,)), dma((groups - 1,)), dma((groups - 1,)),
             dma((devs - 1,)), dma((devs - 1,)), dma((groups - 1,)), dma((groups - 1,)),
             dma((3,)),
         ],
@@ -526,47 +561,32 @@
         name="assemble",
     )(small, joined)
 
-    def exchange(u, plo, phi, collective_id):
-        return pl.pallas_call(
-            functools.partial(halo_kernel, groups, devs),
-            out_shape=ghosts,
-            in_specs=[VMEM] * 3,
-            out_specs=(VMEM,) * 4,
-            scratch_shapes=[dma((4,)), dma((4,))],
-            compiler_params=pltpu.CompilerParams(
-                collective_id=collective_id, has_side_effects=True, vmem_limit_bytes=LIMIT
-            ),
-            name="halo",
-        )(u, plo, phi)
-
-    xlo, xhi, glo, ghi = exchange(u, plo, phi, 1)
-    work = [
-        pltpu.VMEM((BS + 4, FIELDS, YV + 2) + TILE, jnp.float32),
-        pltpu.VMEM((BS + 2, FIELDS, YV) + TILE, jnp.float32),
-        pltpu.VMEM((BS + 1, FIELDS, YV) + TILE, jnp.float32),
-    ] + [pltpu.VMEM((FIELDS, YV + 1) + TILE, jnp.float32)] * 3 + [
-        pltpu.VMEM((FIELDS, YV) + TILE, jnp.float32)
-    ] * 3
-    one, plo, phi = pl.pallas_call(
-        first_kernel,
-        out_shape=(f32(*SLAB), f32(*PACK), f32(*PACK)),
-        in_specs=[VMEM] * 6,
-        out_specs=(VMEM,) * 3,
-        scratch_shapes=work,
-        compiler_params=plain,
-        name="first_stage",
-    )(step, u, xlo, xhi, glo, ghi)
-
-    xlo, xhi, glo, ghi = exchange(one, plo, phi, 2)
+    def vmem(*shape):
+        return pltpu.VMEM(shape, jnp.float32)
+
+    ghosts = [vmem(*EDGE), vmem(*EDGE), vmem(*PACK), vmem(*PACK)]
     out = pl.pallas_call(
-        second_kernel,
+        functools.partial(step_kernel, groups, devs),
         out_shape=f32(BLK_DEV * ROWS, LANES),
-        in_specs=[VMEM] * 7,
+        in_specs=[VMEM] * 4,
         out_specs=VMEM,
-        scratch_shapes=work,
-        compiler_params=plain,
-        name="second_stage",
-    )(step, u, one, xlo, xhi, glo, ghi)
+        scratch_shapes=[
+            vmem(BS + 4, FIELDS, YV + 2, *TILE),
+            vmem(BS + 2, FIELDS, YV, *TILE),
+            vmem(BS + 1, FIELDS, YV, *TILE),
+            vmem(*SLAB),
+            vmem(*SLAB),
+        ] + ghosts + ghosts + ghosts + [vmem(FIELDS, YV + 1, *TILE)] * 3
+        + [vmem(FIELDS, YV, *TILE)] * 3 + [
+            vmem(*TILE), vmem(devs - 1, *TILE), vmem(groups - 1, *TILE), vmem(*TILE),
+            dma((devs - 1,)), dma((devs - 1,)), dma((groups - 1,)), dma((groups - 1,)),
+            dma((4,)), dma((4,)), dma((4,)), dma((4,)),
+        ],
+        compiler_params=pltpu.CompilerParams(
+            collective_id=1, has_side_effects=True, vmem_limit_bytes=LIMIT
+        ),
+        name="step",
+    )(top, u, plo, phi)
     out = out.reshape(BLK_DEV, CHUNKS, FIELDS, LANES).transpose(0, 2, 1, 3)
     return out.reshape(BLK_DEV, FIELDS, CHUNKS * LANES)
 

time: 142 us -> 85.5 us (0.60)
  Pallas kernels: 138 us -> 80.8 us
    pallas_call x4 -> x1, Pallas kernels: 95.6 us -> 45.6 us  [body(): pl.pallas_call(functools.partial(step_kernel, groups, devs), out_shape=f3...]
    pallas_call x1, Pallas kernels: 35.7 us -> 28.8 us  [body(): pl.pallas_call(functools.partial(gather_kernel, groups, devs, cap), out_s...]
    unnamed x2 -> x3, local copies, waits for them, and re-layouts: 2.14 us -> 3.47 us
where the time goes in v3:
time: 85.5 us; the launch traced here: 85 us
  Pallas kernels  80.8 us (95%)
  local copies, waits for them, and re-layouts  3.47 us (4%)
    pallas_call x1, Pallas kernels, body(): pl.pallas_call(functools.partial(step_kernel, groups, devs), out_shape=f3...  45.6 us
    pallas_call x1, Pallas kernels, body(): pl.pallas_call(functools.partial(gather_kernel, groups, devs, cap), out_s...  28.8 us
    pallas_call x1, Pallas kernels, body(): pl.pallas_call(assemble_kernel, out_shape=(f32(*SLAB), f32(*PACK), f32(*P...  3.81 us
    unnamed x3, local copies, waits for them, and re-layouts  3.47 us
    pallas_call x1, Pallas kernels, body(): pl.pallas_call(stage_kernel, out_shape=f32((BLK_DEV - 1) * ROWS, LANES),...  2.67 us

profile of v3, /device:TPU:1, one launch (start us, length us, event | category | flops | bytes accessed | tf_op | source)
XLA Modules:
  0.0 85.0 jit_solution(7188873556241420463)
XLA Ops:
  0.7 0.0 copy-start
  0.7 2.1 %copy-done = f32[31,8,4096]{2,1,0:T(8,128)S(1)} copy-done((f32[31,8,4096]{2,1,0:T(8,128)S(1)}, f32[31,8,4096]{2,1,0:T(8,128)}, u32[]{:S(2)}) %copy-start) | copy-done | bytes 4063256
  2.8 2.7 %stage.1.outgoing = f32[3840,128]{1,0:T(8,128)S(1)} custom-call(s32[1]{0:T(128)S(6)} %copy.4.count_ref, f32[7936,128]{1,0:T(8,128)S(1)} %bitcast.10), custom_call_target="tpu_custom_call" | custom-call | tf_op jit(solution)/shard_map/stage/pallas_call | solution.py:523
  5.5 28.8 %gather.1 = (f32[8,128]{1,0:T(8,128)S(1)}, s32[8,128]{1,0:T(8,128)S(1)}, f32[8192,128]{1,0:T(8,128)}) custom-call(s32[1]{0:T(128)S(6)} %copy.4.count_ref, f32[3840,128]{1,0:T(8,128)S(1)} %stage.1.outgoing, f32[7936,128]{1,0:T(8,128)S(1)} %bitcast.11), custom_call_target="tpu_custom_call" | custom-call | tf_op jit(solution)/shard_map/gather/pallas_call | solution.py:532
  34.2 3.8 %assemble.1 = (f32[16,8,4,8,128]{4,3,2,1,0:T(8,128)S(1)}, f32[16,2,8,128]{3,2,1,0:T(8,128)S(1)}, f32[16,2,8,128]{3,2,1,0:T(8,128)S(1)}) custom-call(s32[8,128]{1,0:T(8,128)S(1)} %get-tuple-element.12.small_ref, f32[8192,128]{1,0:T(8,128)} %get-tuple-element.13.joined), custom_call_target="tpu_custom_call" | custom-call | tf_op jit(solution)/shard_map/assemble/pallas_call | solution.py:555
  38.1 45.6 %step.1 = f32[4096,128]{1,0:T(8,128)S(1)} custom-call(f32[8,128]{1,0:T(8,128)S(1)} %get-tuple-element.11.top_ref, f32[16,8,4,8,128]{4,3,2,1,0:T(8,128)S(1)} %get-tuple-element.14.u_ref, f32[16,2,8,128]{3,2,1,0:T(8,128)S(1)} %get-tuple-element.15.plo, f32[16,2,8,128]{3,2,1,0:T(8,128)S(1)} %get-tuple-element.16.phi), custom_call_target="tpu_custom_call" | custom-call | tf_op jit(solution)/shard_map/step/pallas_call | solution.py:568
  83.6 1.3 %copy.5 = f32[16,8,4096]{2,1,0:T(8,128)} copy(f32[16,8,4096]{2,1,0:T(8,128)S(1)} %bitcast.12) | data formatting | bytes 4194304
Async XLA Ops:
  0.7 2.2 %copy-start = (f32[31,8,4096]{2,1,0:T(8,128)S(1)}, f32[31,8,4096]{2,1,0:T(8,128)}, u32[]{:S(2)}) copy-start(f32[31,8,4096]{2,1,0:T(8,128)} %param.2) | copy-start | bytes 12189700

commit v4 on v3

--- a/solution.py
+++ b/solution.py
@@ -285,20 +285,30 @@
 
 
 def step_kernel(
-    groups, devs, top_ref, u_ref, plo, phi, out_ref,
+    groups, devs, count_ref, own_ref, flat_ref, out_ref,
+    held, flat, outgoing, joined, mine, u_ref, plo, phi,
+    count_msg, row_msg, count_row, count_col, total_ref, small_ref, top_ref,
+    crow_send, crow_recv, ccol_send, ccol_recv, block_sem, local_sem,
     w_ref, sx_ref, fx_ref, acc_ref, one_ref, edge_lo, edge_hi, plo2, phi2,
     xlo, xhi, glo, ghi, xlo2, xhi2, glo2, ghi2, ly, ry, fy, lz, rz, fz,
     speed_msg, speed_row, speed_col, step_ref,
     row_send, row_recv, col_send, col_recv, send, recv, send2, recv2,
 ):
-    g, j, _, _, _, row, column = ring(groups, devs)
-    greet(row + column)
+    staged = pltpu.make_async_copy(own_ref, held, local_sem.at[0])
+    staged.start()
+    g, j, me, curve_next, curve_prev, row, column = ring(groups, devs)
+    greet(row + column + [curve_next, curve_prev])
     up = (lax.rem(g + 1, groups), j)
     down = (lax.rem(g + groups - 1, groups), j)
     right = (g, lax.rem(j + 1, devs))
     left = (g, lax.rem(j + devs - 1, devs))
     speeds = messages(top_ref, speed_row, row_send, row_recv, row)
-    begin(speeds)
+    rebalance(
+        g, j, me, groups * devs, curve_next, count_ref, own_ref, flat_ref, held, flat, outgoing,
+        joined, mine, u_ref, plo, phi, count_msg, row_msg, count_row, count_col, total_ref,
+        small_ref, top_ref, row, column, crow_send, crow_recv, ccol_send, ccol_recv, speeds,
+        block_sem, local_sem, staged,
+    )
     y_copies = [
         remote(phi, glo, send.at[2], recv.at[2], right),
         remote(plo, ghi, send.at[3], recv.at[3], left),
@@ -403,90 +413,93 @@
     return jnp.maximum(jnp.maximum(speeds[0], speeds[1]), speeds[2])
 
 
-def stage_kernel(count_ref, own_ref, out_ref, sem):
-    copies = []
-    for m in range(BLK_DEV - 1):
-        base = jnp.maximum(count_ref[0] - BLK_DEV + 1 + m, 0) * ROWS
-        copies.append(pltpu.make_async_copy(
-            own_ref.at[pl.ds(pl.multiple_of(base, ROWS), ROWS)],
-            out_ref.at[pl.ds(m * ROWS, ROWS)],
-            sem.at[m],
-        ))
-    for copy in copies:
-        copy.start()
-    for copy in copies:
-        copy.wait()
-
-
-def gather_kernel(
-    groups, devs, cap, count_ref, outgoing, own_ref,
-    top_ref, small_ref, joined,
-    count_msg, row_msg, count_row, count_col, total_ref, held,
-    block_sem, row_send, row_recv, col_send, col_recv, local_sem,
+def rebalance(
+    g, j, me, total, curve_next, count_ref, own_ref, flat_ref, held, flat, outgoing, joined,
+    mine, u_ref, plo, phi, count_msg, row_msg, count_row, count_col, total_ref, small_ref, top_ref,
+    row, column, crow_send, crow_recv, ccol_send, ccol_recv, speeds, block_sem, local_sem, staged,
 ):
-    g, j, me, curve_next, curve_prev, row, column = ring(groups, devs)
-    staged = pltpu.make_async_copy(own_ref, held, local_sem.at[2])
-    staged.start()
-    greet(row + column + [curve_next, curve_prev])
+    cap = own_ref.shape[0]
     count = count_ref[0]
     count_msg[...] = jnp.full((8, LANES), count, jnp.int32)
-    counts = messages(count_msg, count_row, row_send, row_recv, row)
+    counts = messages(count_msg, count_row, crow_send, crow_recv, row)
     begin(counts)
+    staged.wait()
+
+    def stage(m, carry):
+        outgoing[m] = held[jnp.clip(count - BLK_DEV + 1 + m, 0, cap - 1)]
+        return carry
+
+    lax.fori_loop(0, BLK_DEV - 1, stage, 0)
     blocks = remote(
-        outgoing, joined.at[pl.ds(ROWS, (BLK_DEV - 1) * ROWS)], block_sem.at[0], block_sem.at[1],
-        curve_next,
+        outgoing, joined.at[pl.ds(1, BLK_DEV - 1)], block_sem.at[0], block_sem.at[1], curve_next
     )
-    blocks.start()
+
+    @pl.when(me < total - 1)
+    def _():
+        blocks.start()
+
+    spare = pltpu.make_async_copy(flat_ref, flat, local_sem.at[1])
+    spare.start()
     local = pltpu.make_async_copy(
-        own_ref.at[pl.ds(0, BLK_DEV * ROWS)], joined.at[pl.ds(BLK_DEV * ROWS, BLK_DEV * ROWS)],
-        local_sem.at[0],
+        own_ref.at[pl.ds(0, BLK_DEV)], joined.at[pl.ds(BLK_DEV, BLK_DEV)], local_sem.at[2]
     )
     local.start()
 
     finish(counts)
     before = jnp.zeros((8, LANES), jnp.int32)
     every = count_msg[...]
-    for d in range(1, devs):
+    for d in range(1, len(row) + 1):
         value = count_row[d - 1]
         every = every + value
         before = before + jnp.where(d <= j, value, 0)
     row_msg[...] = every
-    counts = messages(row_msg, count_col, col_send, col_recv, column)
+    counts = messages(row_msg, count_col, ccol_send, ccol_recv, column)
     begin(counts)
 
-    staged.wait()
+    spare.wait()
     slot = lax.broadcasted_iota(jnp.int32, (8, LANES), 0)
 
     def chunk(t, top):
         for first in list(range(0, cap - 8, 8)) + [cap - 8]:
             u = [
-                held[pl.ds(first * ROWS + t * FIELDS + f, 8, stride=ROWS), :]
+                flat[pl.ds(first * ROWS + t * FIELDS + f, 8, stride=ROWS), :]
                 for f in range(FIELDS)
             ]
             top = jnp.maximum(top, jnp.where(slot + first < count, signal_speed(u), 0.0))
         return top
 
     top_ref[...] = lax.fori_loop(0, CHUNKS, chunk, jnp.zeros((8, LANES), jnp.float32))
+    begin(speeds)
 
     finish(counts)
-    for d in range(1, groups):
+    for d in range(1, len(column) + 1):
         before = before + jnp.where(d <= g, count_col[d - 1], 0)
     total_ref[...] = before - me * BLK_DEV
-    narrow = pltpu.make_async_copy(total_ref, small_ref, local_sem.at[1])
+    narrow = pltpu.make_async_copy(total_ref, small_ref, local_sem.at[3])
     narrow.start()
     narrow.wait()
+    surplus = jnp.clip(small_ref[0, 0], 0, BLK_DEV - 1)
     local.wait()
-    blocks.wait()
-
-
-def assemble_kernel(small_ref, joined, u_ref, plo, phi):
-    surplus = small_ref[0, 0]
+
+    @pl.when(me < total - 1)
+    def _():
+        blocks.wait_send()
+
+    @pl.when(me > 0)
+    def _():
+        blocks.wait_recv()
+
+    def take(k, carry):
+        mine[pl.ds(pl.multiple_of(k * ROWS, ROWS), ROWS), :] = joined[BLK_DEV - surplus + k]
+        return carry
+
+    lax.fori_loop(0, BLK_DEV, take, 0)
 
     def assemble(c, carry):
         for v in range(YV):
             for f in range(FIELDS):
-                base = (BLK_DEV - surplus + (v // 2) * BRICK_Z) * ROWS
-                u_ref[c, f, v] = joined[
+                base = (v // 2) * BRICK_Z * ROWS
+                u_ref[c, f, v] = mine[
                     pl.ds(base + (c * 2 + v % 2) * FIELDS + f, BRICK_Z, stride=ROWS), :
                 ]
         for q, tile in enumerate(pack([u_ref[c, f, 0] for f in range(FIELDS)], 0)):
@@ -502,7 +515,7 @@
 SLAB = (BS, FIELDS, YV) + TILE
 EDGE = (2, FIELDS, YV) + TILE
 PACK = (BS, 2) + TILE
-LIMIT = 48 * 1024 * 1024
+LIMIT = 60 * 1024 * 1024
 
 
 def f32(*shape):
@@ -517,60 +530,34 @@
 def body(groups, devs, blocks_in, counts):
     cap = blocks_in.shape[0]
     rows = blocks_in.reshape(cap, FIELDS, CHUNKS, LANES).transpose(0, 2, 1, 3)
-    rows = rows.reshape(cap * ROWS, LANES)
+    rows = rows.reshape(cap, ROWS, LANES)
     dma = pltpu.SemaphoreType.DMA
-    plain = pltpu.CompilerParams(vmem_limit_bytes=LIMIT)
-    outgoing = pl.pallas_call(
-        stage_kernel,
-        out_shape=f32((BLK_DEV - 1) * ROWS, LANES),
-        in_specs=[SMEM, ANY],
+
+    def vmem(*shape):
+        return pltpu.VMEM(shape, jnp.float32)
+
+    ghosts = [vmem(*EDGE), vmem(*EDGE), vmem(*PACK), vmem(*PACK)]
+    out = pl.pallas_call(
+        functools.partial(step_kernel, groups, devs),
+        out_shape=f32(BLK_DEV * ROWS, LANES),
+        in_specs=[SMEM, ANY, ANY],
         out_specs=VMEM,
-        scratch_shapes=[dma((BLK_DEV - 1,))],
-        compiler_params=plain,
-        name="stage",
-    )(counts, rows)
-    top, small, joined = pl.pallas_call(
-        functools.partial(gather_kernel, groups, devs, cap),
-        out_shape=(
-            f32(*TILE), jax.ShapeDtypeStruct(TILE, jnp.int32), f32(2 * BLK_DEV * ROWS, LANES)
-        ),
-        in_specs=[SMEM, VMEM, ANY],
-        out_specs=(VMEM, SMEM, VMEM),
         scratch_shapes=[
+            vmem(cap, ROWS, LANES),
+            vmem(cap * ROWS, LANES),
+            vmem(BLK_DEV - 1, ROWS, LANES),
+            vmem(2 * BLK_DEV, ROWS, LANES),
+            vmem(BLK_DEV * ROWS, LANES),
+            vmem(*SLAB), vmem(*PACK), vmem(*PACK),
             pltpu.VMEM(TILE, jnp.int32),
             pltpu.VMEM(TILE, jnp.int32),
             pltpu.VMEM((devs - 1,) + TILE, jnp.int32),
             pltpu.VMEM((groups - 1,) + TILE, jnp.int32),
             pltpu.VMEM(TILE, jnp.int32),
-            pltpu.VMEM((cap * ROWS, LANES), jnp.float32),
-            dma((2,)),
+            pltpu.SMEM(TILE, jnp.int32),
+            vmem(*TILE),
             dma((devs - 1,)), dma((devs - 1,)), dma((groups - 1,)), dma((groups - 1,)),
-            dma((3,)),
-        ],
-        compiler_params=pltpu.CompilerParams(
-            collective_id=0, has_side_effects=True, vmem_limit_bytes=LIMIT
-        ),
-        name="gather",
-    )(counts, outgoing, rows)
-    u, plo, phi = pl.pallas_call(
-        assemble_kernel,
-        out_shape=(f32(*SLAB), f32(*PACK), f32(*PACK)),
-        in_specs=[SMEM, VMEM],
-        out_specs=(VMEM,) * 3,
-        compiler_params=plain,
-        name="assemble",
-    )(small, joined)
-
-    def vmem(*shape):
-        return pltpu.VMEM(shape, jnp.float32)
-
-    ghosts = [vmem(*EDGE), vmem(*EDGE), vmem(*PACK), vmem(*PACK)]
-    out = pl.pallas_call(
-        functools.partial(step_kernel, groups, devs),
-        out_shape=f32(BLK_DEV * ROWS, LANES),
-        in_specs=[VMEM] * 4,
-        out_specs=VMEM,
-        scratch_shapes=[
+            dma((2,)), dma((4,)),
             vmem(BS + 4, FIELDS, YV + 2, *TILE),
             vmem(BS + 2, FIELDS, YV, *TILE),
             vmem(BS + 1, FIELDS, YV, *TILE),
@@ -583,10 +570,10 @@
             dma((4,)), dma((4,)), dma((4,)), dma((4,)),
         ],
         compiler_params=pltpu.CompilerParams(
-            collective_id=1, has_side_effects=True, vmem_limit_bytes=LIMIT
+            collective_id=0, has_side_effects=True, vmem_limit_bytes=LIMIT
         ),
         name="step",
-    )(top, u, plo, phi)
+    )(counts, rows, rows.reshape(cap * ROWS, LANES))
     out = out.reshape(BLK_DEV, CHUNKS, FIELDS, LANES).transpose(0, 2, 1, 3)
     return out.reshape(BLK_DEV, FIELDS, CHUNKS * LANES)
 

time: 85.5 us -> 76.1 us (0.89)
  Pallas kernels: 80.8 us -> 72 us
    pallas_call x3 -> x0, Pallas kernels: 35.2 us -> none  [the longest x1 28.8 us: body(): pl.pallas_call(functools.partial(gather_kernel, groups, devs, cap), out_s...]
    pallas_call x1, Pallas kernels: 45.6 us -> 72 us  [body(): pl.pallas_call(functools.partial(step_kernel, groups, devs), out_shape=f3...]
    unnamed x3 -> x1, local copies, waits for them, and re-layouts: 3.47 us -> 3.11 us
where the time goes in v4:
time: 76.1 us; the launch traced here: 75.7 us
  Pallas kernels  72 us (95%)
  local copies, waits for them, and re-layouts  3.11 us (4%)
    pallas_call x1, Pallas kernels, body(): pl.pallas_call(functools.partial(step_kernel, groups, devs), out_shape=f3...  72 us
    unnamed x1, local copies, waits for them, and re-layouts  3.11 us

profile of v4, /device:TPU:1, one launch (start us, length us, event | category | flops | bytes accessed | tf_op | source)
XLA Modules:
  0.0 75.7 jit_solution(10107354172474587886)
XLA Ops:
  0.7 72.0 %step.1 = f32[4096,128]{1,0:T(8,128)} custom-call(s32[1]{0:T(128)S(6)} %copy.4.count_ref, f32[31,256,128]{2,1,0:T(8,128)} %bitcast.12, f32[7936,128]{1,0:T(8,128)} %bitcast.13), custom_call_target="tpu_custom_call" | custom-call | tf_op jit(solution)/shard_map/step/pallas_call | solution.py:540
  72.6 3.1 %copy.5 = f32[16,8,4096]{2,1,0:T(8,128)} copy(f32[16,8,4096]{2,1,0:T(8,128)} %bitcast.14) | data formatting | bytes 4194304

commit v5 on v4

--- a/solution.py
+++ b/solution.py
@@ -122,11 +122,11 @@
     return [x[i] for i in range(x.shape[0])]
 
 
-def fill_planes(source, w_ref, base):
+def fill_planes(source, w_ref, base, v=0, n=YV):
     def one(c, carry):
-        w, _ = primitive([source[c, f] for f in range(FIELDS)])
+        w, _ = primitive([source[c, f, v:v + n] for f in range(FIELDS)])
         for f in range(FIELDS):
-            w_ref[base + c, f, 1:YV + 1] = w[f]
+            w_ref[base + c, f, 1 + v:1 + v + n] = w[f]
         return carry
 
     lax.fori_loop(0, source.shape[0], one, 0)
@@ -197,22 +197,22 @@
     faces(l_ref, r_ref, f_ref, 1, PAIRS + ((YV, 1),))
 
 
-def z_faces(w_ref, c, l_ref, r_ref, f_ref):
+def z_faces(w_ref, c, l_ref, r_ref, f_ref, v, n):
     for f in range(FIELDS):
-        w = w_ref[c + 2, f, 1:YV + 1]
+        w = w_ref[c + 2, f, 1 + v:1 + v + n]
         diff = z_up(split(w)) - w
         slope = half_minmod(z_down(split(diff)), diff)
-        l_ref[f, 0:YV] = w + slope
-        r_ref[f, 0:YV] = z_up(split(w - slope))
-    faces(l_ref, r_ref, f_ref, 2, PAIRS)
-
-
-def z_pass(w_ref, acc_ref, lz, rz, fz):
+        l_ref[f, v:v + n] = w + slope
+        r_ref[f, v:v + n] = z_up(split(w - slope))
+    faces(l_ref, r_ref, f_ref, 2, [(i, 2) for i in range(v, v + n, 2)])
+
+
+def z_pass(w_ref, acc_ref, lz, rz, fz, v=0, n=YV):
     def one(c, carry):
-        z_faces(w_ref, c, lz, rz, fz)
+        z_faces(w_ref, c, lz, rz, fz, v, n)
         for f in range(FIELDS):
-            flux = fz[f]
-            acc_ref[c, f] = flux - z_down(split(flux))
+            flux = fz[f, v:v + n]
+            acc_ref[c, f, v:v + n] = flux - z_down(split(flux))
         return carry
 
     lax.fori_loop(0, BS, one, 0)
@@ -286,7 +286,7 @@
 
 def step_kernel(
     groups, devs, count_ref, own_ref, flat_ref, out_ref,
-    held, flat, outgoing, joined, mine, u_ref, plo, phi,
+    held, flat, outgoing, joined_lo, joined_hi, mine, u_ref, plo, phi,
     count_msg, row_msg, count_row, count_col, total_ref, small_ref, top_ref,
     crow_send, crow_recv, ccol_send, ccol_recv, block_sem, local_sem,
     w_ref, sx_ref, fx_ref, acc_ref, one_ref, edge_lo, edge_hi, plo2, phi2,
@@ -305,9 +305,9 @@
     speeds = messages(top_ref, speed_row, row_send, row_recv, row)
     rebalance(
         g, j, me, groups * devs, curve_next, count_ref, own_ref, flat_ref, held, flat, outgoing,
-        joined, mine, u_ref, plo, phi, count_msg, row_msg, count_row, count_col, total_ref,
+        joined_lo, joined_hi, mine, u_ref, plo, phi, count_msg, row_msg, count_row, count_col, total_ref,
         small_ref, top_ref, row, column, crow_send, crow_recv, ccol_send, ccol_recv, speeds,
-        block_sem, local_sem, staged,
+        block_sem, local_sem, staged, w_ref, acc_ref, lz, rz, fz,
     )
     y_copies = [
         remote(phi, glo, send.at[2], recv.at[2], right),
@@ -320,8 +320,8 @@
     ]
     begin(x_copies)
 
-    fill_planes(u_ref, w_ref, 2)
-    z_pass(w_ref, acc_ref, lz, rz, fz)
+    fill_planes(u_ref, w_ref, 2, 0, 2)
+    z_pass(w_ref, acc_ref, lz, rz, fz, 0, 2)
 
     finish(speeds)
     top = top_ref[...]
@@ -414,9 +414,10 @@
 
 
 def rebalance(
-    g, j, me, total, curve_next, count_ref, own_ref, flat_ref, held, flat, outgoing, joined,
+    g, j, me, total, curve_next, count_ref, own_ref, flat_ref, held, flat, outgoing, joined_lo, joined_hi,
     mine, u_ref, plo, phi, count_msg, row_msg, count_row, count_col, total_ref, small_ref, top_ref,
     row, column, crow_send, crow_recv, ccol_send, ccol_recv, speeds, block_sem, local_sem, staged,
+    w_ref, acc_ref, lz, rz, fz,
 ):
     cap = own_ref.shape[0]
     count = count_ref[0]
@@ -430,20 +431,31 @@
         return carry
 
     lax.fori_loop(0, BLK_DEV - 1, stage, 0)
-    blocks = remote(
-        outgoing, joined.at[pl.ds(1, BLK_DEV - 1)], block_sem.at[0], block_sem.at[1], curve_next
+    early, late = BLK_DEV - BRICK_Z - 1, BRICK_Z
+    upper = remote(
+        outgoing.at[pl.ds(late, early)], joined_hi.at[pl.ds(0, early)],
+        block_sem.at[0], block_sem.at[1], curve_next,
+    )
+    lower = remote(
+        outgoing.at[pl.ds(0, late)], joined_lo.at[pl.ds(0, late)],
+        block_sem.at[2], block_sem.at[3], curve_next,
     )
 
     @pl.when(me < total - 1)
     def _():
-        blocks.start()
+        upper.start()
+        lower.start()
 
     spare = pltpu.make_async_copy(flat_ref, flat, local_sem.at[1])
     spare.start()
-    local = pltpu.make_async_copy(
-        own_ref.at[pl.ds(0, BLK_DEV)], joined.at[pl.ds(BLK_DEV, BLK_DEV)], local_sem.at[2]
-    )
-    local.start()
+    local_hi = pltpu.make_async_copy(
+        own_ref.at[pl.ds(0, BLK_DEV)], joined_hi.at[pl.ds(early, BLK_DEV)], local_sem.at[2]
+    )
+    local_hi.start()
+    local_lo = pltpu.make_async_copy(
+        own_ref.at[pl.ds(0, BRICK_Z)], joined_lo.at[pl.ds(late + early, BRICK_Z)], local_sem.at[4]
+    )
+    local_lo.start()
 
     finish(counts)
     before = jnp.zeros((8, LANES), jnp.int32)
@@ -479,43 +491,65 @@
     narrow.start()
     narrow.wait()
     surplus = jnp.clip(small_ref[0, 0], 0, BLK_DEV - 1)
-    local.wait()
+    first = BLK_DEV - 1 - surplus
+
+    def take(joined, half):
+        def one(k, carry):
+            mine[half, pl.ds(pl.multiple_of(k * ROWS, ROWS), ROWS), :] = joined[first + k]
+            return carry
+
+        lax.fori_loop(0, BRICK_Z, one, 0)
+
+        def assemble(c, carry):
+            for v in (2 * half, 2 * half + 1):
+                for f in range(FIELDS):
+                    u_ref[c, f, v] = mine[
+                        half, pl.ds((c * 2 + v % 2) * FIELDS + f, BRICK_Z, stride=ROWS), :
+                    ]
+            side, edge, target = ((0, 0, plo), (YV - 1, 96, phi))[half]
+            for q, tile in enumerate(pack([u_ref[c, f, side] for f in range(FIELDS)], edge)):
+                target[c, q] = tile
+            return carry
+
+        lax.fori_loop(0, BS, assemble, 0)
+
+    local_hi.wait()
 
     @pl.when(me < total - 1)
     def _():
-        blocks.wait_send()
+        upper.wait_send()
 
     @pl.when(me > 0)
     def _():
-        blocks.wait_recv()
-
-    def take(k, carry):
-        mine[pl.ds(pl.multiple_of(k * ROWS, ROWS), ROWS), :] = joined[BLK_DEV - surplus + k]
-        return carry
-
-    lax.fori_loop(0, BLK_DEV, take, 0)
-
-    def assemble(c, carry):
-        for v in range(YV):
-            for f in range(FIELDS):
-                base = (v // 2) * BRICK_Z * ROWS
-                u_ref[c, f, v] = mine[
-                    pl.ds(base + (c * 2 + v % 2) * FIELDS + f, BRICK_Z, stride=ROWS), :
-                ]
-        for q, tile in enumerate(pack([u_ref[c, f, 0] for f in range(FIELDS)], 0)):
-            plo[c, q] = tile
-        for q, tile in enumerate(pack([u_ref[c, f, YV - 1] for f in range(FIELDS)], 96)):
-            phi[c, q] = tile
-        return carry
-
-    lax.fori_loop(0, BS, assemble, 0)
+        upper.wait_recv()
+
+    shared = pltpu.make_async_copy(
+        joined_hi.at[pl.ds(0, early)], joined_lo.at[pl.ds(late, early)], local_sem.at[5]
+    )
+    shared.start()
+    take(joined_hi, 1)
+    fill_planes(u_ref, w_ref, 2, 2, 2)
+    z_pass(w_ref, acc_ref, lz, rz, fz, 2, 2)
+
+    local_lo.wait()
+    shared.wait()
+
+    @pl.when(me < total - 1)
+    def _():
+        lower.wait_send()
+
+    @pl.when(me > 0)
+    def _():
+        lower.wait_recv()
+
+    take(joined_lo, 0)
 
 
 TILE = (8, LANES)
 SLAB = (BS, FIELDS, YV) + TILE
 EDGE = (2, FIELDS, YV) + TILE
 PACK = (BS, 2) + TILE
-LIMIT = 60 * 1024 * 1024
+LIMIT = 51 * 1024 * 1024
 
 
 def f32(*shape):
@@ -546,8 +580,9 @@
             vmem(cap, ROWS, LANES),
             vmem(cap * ROWS, LANES),
             vmem(BLK_DEV - 1, ROWS, LANES),
-            vmem(2 * BLK_DEV, ROWS, LANES),
-            vmem(BLK_DEV * ROWS, LANES),
+            vmem(BLK_DEV + BRICK_Z - 1, ROWS, LANES),
+            vmem(BLK_DEV + BRICK_Z - 1, ROWS, LANES),
+            vmem(2, BRICK_Z * ROWS, LANES),
             vmem(*SLAB), vmem(*PACK), vmem(*PACK),
             pltpu.VMEM(TILE, jnp.int32),
             pltpu.VMEM(TILE, jnp.int32),
@@ -557,7 +592,7 @@
             pltpu.SMEM(TILE, jnp.int32),
             vmem(*TILE),
             dma((devs - 1,)), dma((devs - 1,)), dma((groups - 1,)), dma((groups - 1,)),
-            dma((2,)), dma((4,)),
+            dma((4,)), dma((6,)),
             vmem(BS + 4, FIELDS, YV + 2, *TILE),
             vmem(BS + 2, FIELDS, YV, *TILE),
             vmem(BS + 1, FIELDS, YV, *TILE),

time: 76.1 us -> 79.7 us (1.047)
  the two profiles are of different devices: /device:TPU:1 before, /device:TPU:15 now
where the time goes in v5:
time: 79.7 us; the launch traced here: 79.5 us
  Pallas kernels  77.5 us (97%)
  local copies, waits for them, and re-layouts  1.32 us (2%)
    pallas_call x1, Pallas kernels, body(): pl.pallas_call(functools.partial(step_kernel, groups, devs), out_shape=f3...  77.5 us

profile of v5, /device:TPU:15, one launch (start us, length us, event | category | flops | bytes accessed | tf_op | source)
XLA Modules:
  0.0 79.5 jit_solution(4117649518415718914)
XLA Ops:
  0.7 77.5 %step.1 = f32[4096,128]{1,0:T(8,128)S(1)} custom-call(s32[1]{0:T(128)S(6)} %copy.4.count_ref, f32[31,256,128]{2,1,0:T(8,128)} %bitcast.13, f32[7936,128]{1,0:T(8,128)} %bitcast.14), custom_call_target="tpu_custom_call" | custom-call | tf_op jit(solution)/shard_map/step/pallas_call | solution.py:574
  78.2 1.3 %copy.5 = f32[16,8,4096]{2,1,0:T(8,128)} copy(f32[16,8,4096]{2,1,0:T(8,128)S(1)} %bitcast.12) | data formatting | bytes 4194304

commit v6 on v4

--- a/solution.py
+++ b/solution.py
@@ -172,15 +172,15 @@
     lax.fori_loop(0, BS + 1, one, 0)
 
 
-def faces(l_ref, r_ref, f_ref, n, parts):
-    for v, size in parts:
+def faces(l_ref, r_ref, f_ref, n):
+    for v, size in PAIRS:
         left = [l_ref[f, v:v + size] for f in range(FIELDS)]
         right = [r_ref[f, v:v + size] for f in range(FIELDS)]
         for f, flux in enumerate(hlle(left, right, n)):
             f_ref[f, v:v + size] = flux
 
 
-def y_faces(w_ref, c, l_ref, r_ref, f_ref):
+def y_states(w_ref, c, l_ref, r_ref):
     lane = lax.broadcasted_iota(jnp.int32, (YV + 2, 8, LANES), 2)
     top = lane >= LANES - BS
     bottom = lane < BS
@@ -194,43 +194,54 @@
         low = roll(w - slope, -BS, 2)
         l_ref[f] = (w + slope)[:YV + 1]
         r_ref[f] = jnp.where(top[1:], low[1:], low[:-1])
-    faces(l_ref, r_ref, f_ref, 1, PAIRS + ((YV, 1),))
-
-
-def z_faces(w_ref, c, l_ref, r_ref, f_ref):
+
+
+def z_states(w_ref, c, l_ref, r_ref):
     for f in range(FIELDS):
         w = w_ref[c + 2, f, 1:YV + 1]
         diff = z_up(split(w)) - w
         slope = half_minmod(z_down(split(diff)), diff)
-        l_ref[f, 0:YV] = w + slope
-        r_ref[f, 0:YV] = z_up(split(w - slope))
-    faces(l_ref, r_ref, f_ref, 2, PAIRS)
+        l_ref[f] = w + slope
+        r_ref[f] = z_up(split(w - slope))
 
 
 def z_pass(w_ref, acc_ref, lz, rz, fz):
-    def one(c, carry):
-        z_faces(w_ref, c, lz, rz, fz)
-        for f in range(FIELDS):
-            flux = fz[f]
-            acc_ref[c, f] = flux - z_down(split(flux))
-        return carry
-
-    lax.fori_loop(0, BS, one, 0)
+    def two(i, carry):
+        for p in range(2):
+            z_states(w_ref, 2 * i + p, lz.at[p], rz.at[p])
+        for p in range(2):
+            faces(lz.at[p], rz.at[p], fz.at[p], 2)
+        for p in range(2):
+            for f in range(FIELDS):
+                flux = fz[p, f]
+                acc_ref[2 * i + p, f] = flux - z_down(split(flux))
+        return carry
+
+    lax.fori_loop(0, BS // 2, two, 0)
 
 
 def y_pass(w_ref, acc_ref, ly, ry, fy):
     bottom = lax.broadcasted_iota(jnp.int32, (YV, 8, LANES), 2) < BS
 
-    def one(c, carry):
-        y_faces(w_ref, c, ly, ry, fy)
-        for f in range(FIELDS):
-            flux = fy[f]
-            rolled = roll(flux, BS, 2)
-            across = flux[1:] - jnp.where(bottom, rolled[:-1], rolled[1:])
-            acc_ref[c, f] = across + acc_ref[c, f]
-        return carry
-
-    lax.fori_loop(0, BS, one, 0)
+    def two(i, carry):
+        for p in range(2):
+            y_states(w_ref, 2 * i + p, ly.at[p], ry.at[p])
+        left = [jnp.stack([ly[p, f, YV] for p in range(2)]) for f in range(FIELDS)]
+        right = [jnp.stack([ry[p, f, YV] for p in range(2)]) for f in range(FIELDS)]
+        for f, flux in enumerate(hlle(left, right, 1)):
+            for p in range(2):
+                fy[p, f, YV] = flux[p]
+        for p in range(2):
+            faces(ly.at[p], ry.at[p], fy.at[p], 1)
+        for p in range(2):
+            for f in range(FIELDS):
+                flux = fy[p, f]
+                rolled = roll(flux, BS, 2)
+                across = flux[1:] - jnp.where(bottom, rolled[:-1], rolled[1:])
+                acc_ref[2 * i + p, f] = across + acc_ref[2 * i + p, f]
+        return carry
+
+    lax.fori_loop(0, BS // 2, two, 0)
 
 
 def pack(tiles, base):
@@ -515,7 +526,7 @@
 SLAB = (BS, FIELDS, YV) + TILE
 EDGE = (2, FIELDS, YV) + TILE
 PACK = (BS, 2) + TILE
-LIMIT = 60 * 1024 * 1024
+LIMIT = 51 * 1024 * 1024
 
 
 def f32(*shape):
@@ -563,8 +574,8 @@
             vmem(BS + 1, FIELDS, YV, *TILE),
             vmem(*SLAB),
             vmem(*SLAB),
-        ] + ghosts + ghosts + ghosts + [vmem(FIELDS, YV + 1, *TILE)] * 3
-        + [vmem(FIELDS, YV, *TILE)] * 3 + [
+        ] + ghosts + ghosts + ghosts + [vmem(2, FIELDS, YV + 1, *TILE)] * 3
+        + [vmem(2, FIELDS, YV, *TILE)] * 3 + [
             vmem(*TILE), vmem(devs - 1, *TILE), vmem(groups - 1, *TILE), vmem(*TILE),
             dma((devs - 1,)), dma((devs - 1,)), dma((groups - 1,)), dma((groups - 1,)),
             dma((4,)), dma((4,)), dma((4,)), dma((4,)),

time: 76.1 us -> 82.1 us (1.079)
  Pallas kernels: 72 us -> 79.8 us
  local copies, waits for them, and re-layouts: 3.11 us -> 1.32 us
    pallas_call x1, Pallas kernels: 72 us -> 79.8 us  [body(): pl.pallas_call(functools.partial(step_kernel, groups, devs), out_shape=f3...]
    unnamed x1, local copies, waits for them, and re-layouts: 3.11 us -> 1.32 us
where the time goes in v6:
time: 82.1 us; the launch traced here: 81.8 us
  Pallas kernels  79.8 us (97%)
  local copies, waits for them, and re-layouts  1.32 us (2%)
    pallas_call x1, Pallas kernels, body(): pl.pallas_call(functools.partial(step_kernel, groups, devs), out_shape=f3...  79.8 us

profile of v6, /device:TPU:1, one launch (start us, length us, event | category | flops | bytes accessed | tf_op | source)
XLA Modules:
  0.0 81.8 jit_solution(1313024395144875801)
XLA Ops:
  0.7 79.8 %step.1 = f32[4096,128]{1,0:T(8,128)S(1)} custom-call(s32[1]{0:T(128)S(6)} %copy.4.count_ref, f32[31,256,128]{2,1,0:T(8,128)} %bitcast.13, f32[7936,128]{1,0:T(8,128)} %bitcast.14), custom_call_target="tpu_custom_call" | custom-call | tf_op jit(solution)/shard_map/step/pallas_call | solution.py:551
  80.5 1.3 %copy.5 = f32[16,8,4096]{2,1,0:T(8,128)} copy(f32[16,8,4096]{2,1,0:T(8,128)S(1)} %bitcast.12) | data formatting | bytes 4194304
